TPU v7x, 128 devices: a whole 4x4x4 slice. The times are simulated.
128 devices in a mesh: row: 8 (over z, y_hi), col: 16 (over y_lo, x, core).
Axes of the slice: x: 4, y: 4 (y_hi: 2, y_lo: 2; y = y_hi * 2 + y_lo), z: 4, core: 2. Of those that a mesh axis runs over, the one named last changes fastest.
Arguments:
- coarse_latent: bfloat16 [320, 128, 256], P(None, ('row', 'col')), may hold values from -6 to 6
- fine_latent: bfloat16 [512, 327680], P('row', 'col'), may hold values from -6 to 6
- timestep: int32 [1], replicated, may hold values from 12 to 19
- coarse_first: bfloat16 [3, 3, 320, 320], replicated, may hold values from -0.1875 to 0.1875
- coarse_second: bfloat16 [3, 3, 320, 320], replicated, may hold values from -0.1875 to 0.1875
- local_weight: bfloat16 [3, 3, 320, 320], replicated, may hold values from -0.1875 to 0.1875
- dilated_weight: bfloat16 [3, 3, 320, 320], replicated, may hold values from -0.1875 to 0.1875
Outputs:
- blended: float32 [512, 327680], P('row', 'col')
All inputs are finite; a program needn't handle non-finite values.
Results may differ from a plain program's by a relative error of at most 0.0025.
Values may be sent and summed in bfloat16 or wider, within the bound.
A program may use at most 320 MiB of HBM per device.

v0:
```python
import functools
import math

import jax
import jax.numpy as jnp
from jax import lax
from jax.experimental import pallas as pl
from jax.experimental.pallas import tpu as pltpu
from jax.sharding import PartitionSpec as P

STEPS = 50
C = 320
ROWS = 8
COLS = 16
PAIR = 2 * C
TALL = 64
PAIRS = 32
CHUNK = 8
CELLS = CHUNK * TALL
SHIFTS = (-4, -1, 0, 1, 4)
KEYS = 6144
PITCH = 20
MESH = pl.DeviceIdType.MESH
VMEM_LIMIT = 60 * 1024 * 1024


def silu(x):
    return x / (1.0 + jnp.exp(-x))


def exchange_kernel(
    fine, coarse, left, right, top, bottom, top_left, top_right, bottom_left, bottom_right, patch,
    rows_in, packed, zero_side, zero_flat, zero_patch, local_sem, send_sem, recv_sem, patch_send, patch_recv,
):
    r = lax.axis_index("row")
    c = lax.axis_index("col")

    def at(dr, dc):
        return (r + dr, c + dc)

    def present(dr, dc):
        ok = None
        for cond, need in ((r > 0, dr < 0), (r < ROWS - 1, dr > 0), (c > 0, dc < 0), (c < COLS - 1, dc > 0)):
            if need:
                ok = cond if ok is None else jnp.logical_and(ok, cond)
        return ok

    barrier = pltpu.get_barrier_semaphore()

    def greet(dev):
        pl.semaphore_signal(barrier, inc=1, device_id=dev, device_id_type=MESH)

    above = r > 0
    below = r < ROWS - 1

    def greet_row(step, _):
        other = lax.rem(c + step, COLS)
        greet((r, other))
        return 0

    lax.fori_loop(1, COLS, greet_row, 0)
    ndiag = ((-1, -1), (-1, 0), (-1, 1), (1, -1), (1, 0), (1, 1))

    def greet_all(dr, cond):
        @pl.when(cond)
        def _():
            def one(step, _):
                greet((r + dr, step))
                return 0
            lax.fori_loop(0, COLS, one, 0)

    greet_all(-1, above)
    greet_all(1, below)
    expected = COLS - 1 + jnp.where(above, COLS, 0) + jnp.where(below, COLS, 0)
    load_top = pltpu.make_async_copy(fine.at[pl.ds(0, 16), :], rows_in.at[0], local_sem.at[0])
    load_low = pltpu.make_async_copy(fine.at[pl.ds(48, 16), :], rows_in.at[1], local_sem.at[1])
    load_top.start()
    load_low.start()
    zero_side[...] = jnp.zeros_like(zero_side)
    zero_flat[...] = jnp.zeros_like(zero_flat)
    zero_patch[...] = jnp.zeros_like(zero_patch)
    load_top.wait()
    load_low.wait()
    for slot, first in ((0, 0), (1, 12)):
        for g in range(4):
            block = rows_in[slot, :, 5120 * g : 5120 * (g + 1)].astype(jnp.float32)
            packed[slot, 4 * g : 4 * g + 4, :] = block[first : first + 4]
    pieces = packed[...].astype(jnp.bfloat16)
    rows_in[0, :, 0:5120] = pieces[0]
    rows_in[1, :, 0:5120] = pieces[1]
    pl.semaphore_wait(barrier, expected)

    sides = (
        ((0, 1), fine.at[:, pl.ds(20480 - 1280, 1280)], left, 0, zero_side),
        ((0, -1), fine.at[:, pl.ds(0, 1280)], right, 1, zero_side),
        ((1, 0), rows_in.at[1, :, pl.ds(0, 5120)], top, 2, zero_flat),
        ((-1, 0), rows_in.at[0, :, pl.ds(0, 5120)], bottom, 3, zero_flat),
        ((1, 1), fine.at[pl.ds(48, 16), pl.ds(20480 - 1280, 1280)], top_left, 4, zero_side.at[pl.ds(0, 16), :]),
        ((1, -1), fine.at[pl.ds(48, 16), pl.ds(0, 1280)], top_right, 5, zero_side.at[pl.ds(0, 16), :]),
        ((-1, 1), fine.at[pl.ds(0, 16), pl.ds(20480 - 1280, 1280)], bottom_left, 6, zero_side.at[pl.ds(0, 16), :]),
        ((-1, -1), fine.at[pl.ds(0, 16), pl.ds(0, 1280)], bottom_right, 7, zero_side.at[pl.ds(0, 16), :]),
    )

    def side_copy(step, src, dst, k):
        return pltpu.make_async_remote_copy(
            src_ref=src, dst_ref=dst, send_sem=send_sem.at[k], recv_sem=recv_sem.at[k],
            device_id=at(*step), device_id_type=MESH)

    for step, src, dst, k, zero in sides:
        @pl.when(present(*step))
        def _(step=step, src=src, dst=dst, k=k):
            side_copy(step, src, dst, k).start()

        @pl.when(jnp.logical_not(present(-step[0], -step[1])))
        def _(dst=dst, k=k, zero=zero):
            pltpu.make_async_copy(zero, dst, recv_sem.at[k]).start()

    def window(target):
        return coarse.at[pl.ds(pl.multiple_of(16 * target, 16), 32), :]

    def patch_copy(dev_r, dev_c, k, slot):
        return pltpu.make_async_remote_copy(
            src_ref=window(dev_c), dst_ref=patch.at[k], send_sem=patch_send.at[slot, dev_c],
            recv_sem=patch_recv.at[k], device_id=(dev_r, dev_c), device_id_type=MESH)

    own = pltpu.make_async_copy(window(c), patch.at[c + 3], patch_recv.at[c + 3])
    own.start()

    def send_row(step, _):
        patch_copy(r, lax.rem(c + step, COLS), c + 3, 0).start()
        return 0

    lax.fori_loop(1, COLS, send_row, 0)
    down = jnp.logical_and(below, c >= 13)
    up = jnp.logical_and(above, c < 3)

    @pl.when(down)
    def _():
        def one(step, _):
            patch_copy(r + 1, lax.rem(c + step, COLS), c - 13, 1).start()
            return 0
        lax.fori_loop(0, COLS, one, 0)

    @pl.when(up)
    def _():
        def one(step, _):
            patch_copy(r - 1, lax.rem(c + step, COLS), c + 19, 1).start()
            return 0
        lax.fori_loop(0, COLS, one, 0)

    for k in (0, 1, 2):
        @pl.when(jnp.logical_not(above))
        def _(k=k):
            pltpu.make_async_copy(zero_patch, patch.at[k], patch_recv.at[k]).start()
    for k in (19, 20, 21):
        @pl.when(jnp.logical_not(below))
        def _(k=k):
            pltpu.make_async_copy(zero_patch, patch.at[k], patch_recv.at[k]).start()

    for step, src, dst, k, zero in sides:
        pltpu.make_async_copy(zero, dst, recv_sem.at[k]).wait()

    def got(k, _):
        pltpu.make_async_copy(zero_patch, patch.at[k], patch_recv.at[k]).wait()
        return 0

    lax.fori_loop(0, 22, got, 0)
    for step, src, dst, k, zero in sides:
        @pl.when(present(*step))
        def _(step=step, src=src, dst=dst, k=k):
            side_copy(step, src, dst, k).wait_send()

    def sent_row(step, _):
        patch_copy(r, lax.rem(c + step, COLS), c + 3, 0).wait_send()
        return 0

    lax.fori_loop(1, COLS, sent_row, 0)

    @pl.when(down)
    def _():
        def one(step, _):
            patch_copy(r + 1, lax.rem(c + step, COLS), c - 13, 1).wait_send()
            return 0
        lax.fori_loop(0, COLS, one, 0)

    @pl.when(up)
    def _():
        def one(step, _):
            patch_copy(r - 1, lax.rem(c + step, COLS), c + 19, 1).wait_send()
            return 0
        lax.fori_loop(0, COLS, one, 0)


def exchange(fine, coarse):
    bf = jnp.bfloat16
    side = jax.ShapeDtypeStruct((64, 1280), bf)
    flat = jax.ShapeDtypeStruct((16, 5120), bf)
    corner = jax.ShapeDtypeStruct((16, 1280), bf)
    return pl.pallas_call(
        exchange_kernel,
        out_shape=(side, side, flat, flat, corner, corner, corner, corner, jax.ShapeDtypeStruct((22, 32, 384), bf)),
        in_specs=[pl.BlockSpec(memory_space=pl.ANY)] * 2,
        out_specs=[pl.BlockSpec(memory_space=pl.ANY)] * 9,
        scratch_shapes=[
            pltpu.VMEM((2, 16, 20480), bf),
            pltpu.VMEM((2, 16, 5120), jnp.float32),
            pltpu.VMEM((64, 1280), bf),
            pltpu.VMEM((16, 5120), bf),
            pltpu.VMEM((32, 384), bf),
            pltpu.SemaphoreType.DMA((2,)),
            pltpu.SemaphoreType.DMA((8,)),
            pltpu.SemaphoreType.DMA((8,)),
            pltpu.SemaphoreType.DMA((2, COLS)),
            pltpu.SemaphoreType.DMA((22,)),
        ],
        compiler_params=pltpu.CompilerParams(collective_id=0, has_side_effects=True, vmem_limit_bytes=32 * 1024 * 1024),
        name="exchange",
    )(fine, coarse)


def tap_pieces(parity):
    out = []
    for s in (1, 2, 3):
        if parity == 0:
            out += [(s, -1, 2, 3), (s, 0, 0, 5)]
        else:
            out += [(s, 0, 0, 5), (s, 1, 0, 3)]
    first = 0 if parity == 0 else 2
    for s in (0, 2, 4):
        for off in (-2, 0, 2):
            if s == 2 and off == 0:
                continue
            out.append((s, off, first, 3))
    return out


def local_kernel(
    where, params, fine, left, right, top, bottom, top_left, top_right, bottom_left, bottom_right, patch,
    coarse_first, coarse_second, local_weight, dilated_weight, out,
    raw, shifted, taps_raw, taps, first_taps, second_taps, hal_top, hal_low, edges, corners, lifted,
    patch_in, grid_act, grid_raw, cells1, cells2, cells3, keys1, keys2, turned, blocks, acc, staged,
    in_sem, w_sem, out_sem,
):
    f32, bf = jnp.float32, jnp.bfloat16
    r, c = where()
    ratio, lift, keep, gain = params[0], params[1], params[2], params[3]

    loads = []

    def load(src, dst, k):
        cp = pltpu.make_async_copy(src, dst, in_sem.at[k])
        cp.start()
        loads.append(cp)

    for p in range(PAIRS):
        load(fine.at[:, pl.ds(PAIR * p, PAIR)], raw.at[p + 2], p)
    for p in range(2):
        load(left.at[:, pl.ds(PAIR * p, PAIR)], raw.at[p], 32 + p)
        load(right.at[:, pl.ds(PAIR * p, PAIR)], raw.at[34 + p], 34 + p)
    load(top, edges.at[0], 36)
    load(bottom, edges.at[1], 37)
    for k, ref in enumerate((top_left, top_right, bottom_left, bottom_right)):
        load(ref, corners.at[k], 38 + k)
    load(patch, patch_in, 42)
    w_loads = []
    for k, ref in enumerate((dilated_weight, local_weight, coarse_first, coarse_second)):
        cp = pltpu.make_async_copy(ref, taps_raw.at[k], w_sem.at[k])
        cp.start()
        w_loads.append(cp)
    for cp in loads:
        cp.wait()

    hal_top[...] = jnp.zeros_like(hal_top)
    hal_low[...] = jnp.zeros_like(hal_low)
    for slot, ref, base in ((0, hal_top, 4), (1, hal_low, 0)):
        for p in range(PAIRS):
            g, q = p // 8, p % 8
            block = edges[slot, :, PAIR * q : PAIR * (q + 1)].astype(f32)
            ref[p + 2, base : base + 4, :] = block[4 * g : 4 * g + 4]
    for p in range(2):
        lanes = slice(PAIR * p, PAIR * (p + 1))
        hal_top[p, 4:8, :] = corners[0, :, lanes].astype(f32)[12:16]
        hal_top[34 + p, 4:8, :] = corners[1, :, lanes].astype(f32)[12:16]
        hal_low[p, 0:4, :] = corners[2, :, lanes].astype(f32)[0:4]
        hal_low[34 + p, 0:4, :] = corners[3, :, lanes].astype(f32)[0:4]

    def prepare(p, _):
        lifted[0:8, :] = silu(hal_top[p])
        lifted[8:72, :] = silu(raw[p].astype(f32))
        lifted[72:80, :] = silu(hal_low[p])
        for k, s in enumerate(SHIFTS):
            shifted[k, p] = lifted[8 + s : 72 + s, :].astype(bf)
        return 0

    lax.fori_loop(0, PAIRS + 4, prepare, 0)

    for cp in w_loads:
        cp.wait()
    gap = jnp.zeros((C, 64), bf)
    dilated = lambda a, b: taps_raw[0, 3 * a + b]
    local = lambda a, b: (ratio * taps_raw[1, 3 * a + b].astype(f32)).astype(bf)
    for par in range(2):
        at = 0
        for a in range(3):
            row = []
            for b in range(3):
                if a == 1 and b == 1:
                    row.append((dilated(1, 1).astype(f32) + ratio * taps_raw[1, 4].astype(f32)).astype(bf))
                else:
                    row.append(local(a, b))
            row = [gap] + row if par == 0 else row + [gap]
            taps[par, :, at : at + 1024] = jnp.concatenate(row, axis=1)
            at += 1024
        for a in range(3):
            for b in range(3):
                if a == 1 and b == 1:
                    continue
                w = dilated(a, b)
                taps[par, :, at : at + 384] = jnp.concatenate([w, gap] if par == 0 else [gap, w], axis=1)
                at += 384
    for k in range(9):
        first_taps[:, 384 * k : 384 * k + 384] = jnp.concatenate([taps_raw[2, k], gap], axis=1)
        second_taps[:, 384 * k : 384 * k + 384] = jnp.concatenate([taps_raw[3, k], gap], axis=1)
    eye = lax.broadcasted_iota(jnp.int32, (C, 384), 0) == lax.broadcasted_iota(jnp.int32, (C, 384), 1)
    second_taps[:, 3456:3840] = eye.astype(f32).astype(bf)

    values = patch_in[...].astype(f32).reshape(22 * 32, 384)
    for t in range(3):
        part = values[:, 128 * t : 128 * t + 128]
        grid_raw[t] = part
        grid_act[t] = silu(part)
    cells1[...] = jnp.zeros_like(cells1)
    cells2[...] = jnp.zeros_like(cells2)
    cells3[...] = jnp.zeros_like(cells3)
    for t in range(3):
        lanes = slice(128 * t, 128 * t + 128)
        for m in range(22):
            cells1[24 * m : 24 * m + 22, lanes] = grid_act[t, pl.ds(m + 1, 22, stride=32), :]
        for m in range(18):
            cells3[PITCH * m : PITCH * m + PITCH, lanes] = grid_raw[t, pl.ds(64 + m + 3, PITCH, stride=32), :]
    for a in range(3):
        for b in range(3):
            k = 3 * a + b
            first = 24 * b + a
            keys1[:, 384 * k : 384 * k + 384] = cells1[first : first + 512, :].astype(bf)
    contract = (((1,), (1,)), ((), ()))
    hidden = lax.dot_general(first_taps[...], keys1[...], contract, preferred_element_type=f32)
    hidden = jnp.concatenate([silu(hidden), jnp.zeros((64, 512), f32)], axis=0)
    turned[...] = jnp.transpose(hidden)
    field_row = lax.broadcasted_iota(jnp.int32, (PITCH, 384), 0) + (16 * r - 2)
    row_ok = jnp.logical_and(field_row >= 0, field_row < 128)
    for m in range(20):
        col = 16 * c - 2 + m
        ok = jnp.logical_and(row_ok, jnp.logical_and(col >= 0, col < 256))
        cells2[PITCH * m : PITCH * m + PITCH, :] = jnp.where(ok, turned[24 * m : 24 * m + PITCH, :], 0.0)
    for a in range(3):
        for b in range(3):
            k = 3 * a + b
            first = PITCH * b + a
            keys2[:, 384 * k : 384 * k + 384] = cells2[first : first + 384, :].astype(bf)
    keys2[:, 3456:3840] = cells3[...].astype(bf)
    coarse = lift * lax.dot_general(second_taps[...], keys2[...], contract, preferred_element_type=f32)
    for q in range(4):
        part = coarse if q == 0 else pltpu.roll(coarse, 384 - 80 * q, axis=1)
        part = part[:, 0:128]
        high = part.astype(bf)
        blocks[q, :, 0:128] = high
        blocks[q, :, 128:256] = (part - high.astype(f32)).astype(bf)

    lane = lax.broadcasted_iota(jnp.int32, (TALL, 128), 1)
    group = jnp.zeros((TALL, 128), jnp.int32)
    for t in range(1, 7):
        group = group + (lane >= PITCH * t).astype(jnp.int32)
    lane_row = (lane - PITCH * group + (16 * r - 1)).astype(f32)
    lane_col = (group + (16 * c - 1)).astype(f32)
    fine_row = (lax.broadcasted_iota(jnp.int32, (TALL, 128), 0) + 64 * r).astype(f32)
    where_row = jnp.clip((fine_row + 0.5) * 0.25 - 0.5, 0.0, 127.0)
    row_share = jnp.maximum(1.0 - jnp.abs(where_row - lane_row), 0.0)
    base_col = (jnp.zeros((TALL, 128), jnp.int32) + 64 * c).astype(f32)

    def shares(q, par):
        out = []
        for pp in range(CHUNK):
            spot = jnp.clip((base_col + (16 * q + 2 * pp + par + 0.5)) * 0.25 - 0.5, 0.0, 255.0)
            part = row_share * jnp.maximum(1.0 - jnp.abs(spot - (lane_col + 4 * q)), 0.0)
            out.append(jnp.concatenate([part, part], axis=1).astype(bf))
        return jnp.concatenate(out, axis=0)

    pending = [None, None]
    for q in range(4):
        for par in range(2):
            pieces = []
            for s, off, tile, n in tap_pieces(par):
                first = 2 + CHUNK * q + off
                part = shifted[s, first : first + CHUNK, :, 128 * tile : 128 * (tile + n)]
                pieces.append(part.reshape(CELLS, 128 * n))
            pieces.append(shares(q, par))
            rhs = jnp.concatenate(pieces, axis=1)
            lhs = jnp.concatenate([taps[par], blocks[q]], axis=1)
            acc[C * par : C * par + C, :] = lax.dot_general(lhs, rhs, contract, preferred_element_type=f32)
        slot = q % 2
        if pending[slot] is not None:
            pending[slot].wait()
        for u in range(CHUNK // 2):
            block = jnp.transpose(acc[:, 128 * u : 128 * u + 128])
            for v in range(2):
                pp = 2 * u + v
                cells = raw[2 + CHUNK * q + pp].astype(f32)
                staged[slot, :, PAIR * pp : PAIR * (pp + 1)] = keep * cells + gain * block[64 * v : 64 * v + 64]
        cp = pltpu.make_async_copy(staged.at[slot], out.at[:, pl.ds(5120 * q, 5120)], out_sem.at[slot])
        cp.start()
        pending[slot] = cp
    for cp in pending:
        cp.wait()


def local_work(where, params, *arrays):
    f32, bf = jnp.float32, jnp.bfloat16
    any_spec = pl.BlockSpec(memory_space=pl.ANY)
    return pl.pallas_call(
        functools.partial(local_kernel, where),
        out_shape=jax.ShapeDtypeStruct((64, 20480), f32),
        in_specs=[pl.BlockSpec(memory_space=pltpu.SMEM)] + [any_spec] * len(arrays),
        out_specs=any_spec,
        scratch_shapes=[
            pltpu.VMEM((36, 64, 640), bf),
            pltpu.VMEM((5, 36, 64, 640), bf),
            pltpu.VMEM((4, 9, C, C), bf),
            pltpu.VMEM((2, C, KEYS), bf),
            pltpu.VMEM((C, 3456), bf),
            pltpu.VMEM((C, 3840), bf),
            pltpu.VMEM((36, 8, 640), f32),
            pltpu.VMEM((36, 8, 640), f32),
            pltpu.VMEM((2, 16, 5120), bf),
            pltpu.VMEM((4, 16, 1280), bf),
            pltpu.VMEM((80, 640), f32),
            pltpu.VMEM((22, 32, 384), bf),
            pltpu.VMEM((3, 704, 128), f32),
            pltpu.VMEM((3, 704, 128), f32),
            pltpu.VMEM((568, 384), f32),
            pltpu.VMEM((432, 384), f32),
            pltpu.VMEM((384, 384), f32),
            pltpu.VMEM((512, 3456), bf),
            pltpu.VMEM((384, 3840), bf),
            pltpu.VMEM((512, 384), f32),
            pltpu.VMEM((4, C, 256), bf),
            pltpu.VMEM((PAIR, CELLS), f32),
            pltpu.VMEM((2, 64, 5120), f32),
            pltpu.SemaphoreType.DMA((43,)),
            pltpu.SemaphoreType.DMA((4,)),
            pltpu.SemaphoreType.DMA((2,)),
        ],
        compiler_params=pltpu.CompilerParams(vmem_limit_bytes=VMEM_LIMIT),
        name="local_work",
    )(params, *arrays)


def blend_params(timestep):
    mix = (1.0 + jnp.cos(math.pi * timestep[0].astype(jnp.float32) / STEPS)) / 2.0
    skip = mix**3
    gain = (1.0 - skip) * mix
    return jnp.stack([(1.0 - mix) / mix, skip / gain, 1.0 - skip, gain])


def on_device(coarse_latent, fine_latent, timestep, coarse_first, coarse_second, local_weight, dilated_weight):
    row = jnp.transpose(coarse_latent.reshape(C, 256))
    row = jnp.pad(row, ((4, 28), (0, 64)))
    halos = exchange(fine_latent, row)
    flat = lambda w: w.reshape(9, C, C)
    return local_work(
        lambda: (lax.axis_index("row"), lax.axis_index("col")),
        blend_params(timestep), fine_latent, *halos,
        flat(coarse_first), flat(coarse_second), flat(local_weight), flat(dilated_weight))


def solution(mesh):
    placed = (P(None, ("row", "col"), None), P("row", "col"), P(), P(), P(), P(), P())
    return jax.shard_map(
        on_device, mesh=mesh, in_specs=placed, out_specs=P("row", "col"), check_vma=False
    )
```

profile of v0, /device:TPU:1, one launch (start us, length us, event | category | flops | bytes accessed | tf_op | source)
XLA Modules:
  0.0 73.1 jit_solution(3510741814743761003)
XLA Ops:
  0.8 0.6 pad_maximum_fusion.params
  1.4 1.1 %copy.8 = bf16[320,1,256]{0,2,1:T(8,128)(2,1)S(1)} copy(bf16[320,1,256]{2,0,1:T(8,128)(2,1)} %param.7) | data formatting | bytes 327680 | tf_op args[0]
  2.5 0.1 pad.4.coarse
  2.6 0.0 copy-start
  2.6 1.7 %copy-done = bf16[64,20480]{1,0:T(8,128)(2,1)S(1)} copy-done((bf16[64,20480]{1,0:T(8,128)(2,1)S(1)}, bf16[64,20480]{1,0:T(8,128)(2,1)}, u32[]{:S(2)}) %copy-start) | copy-done | bytes 2621464
  4.3 27.8 %exchange.1 = (bf16[64,1280]{1,0:T(8,128)(2,1)S(1)}, bf16[64,1280]{1,0:T(8,128)(2,1)S(1)}, bf16[16,5120]{1,0:T(8,128)(2,1)S(1)}, bf16[16,5120]{1,0:T(8,128)(2,1)...) custom-call(bf16[64,20480]{1,0:T(8,128)(2,1)S(1)} %copy-done, ...), custom_call_target="tpu_custom_call" | custom-call | tf_op jit(solution)/shard_map/exchange/pallas_call | solution.py:199
  32.1 0.0 copy-start.1
  32.1 0.8 %copy-done.1 = bf16[22,32,384]{2,1,0:T(8,128)(2,1)} copy-done((bf16[22,32,384]{2,1,0:T(8,128)(2,1)}, bf16[22,32,384]{2,1,0:T(8,128)(2,1)S(1)}, u32[]{:S(2)}) %copy-start.1) | copy-done | bytes 540696
  32.9 0.0 copy-start.2
  32.9 0.7 copy-done.2
  33.6 0.0 copy-start.3
  33.6 0.7 copy-done.3
  34.3 0.0 copy-start.4
  34.3 0.7 copy-done.4
  34.9 0.0 copy-start.5
  34.9 0.7 copy-done.5
  35.6 0.0 copy-start.6
  35.6 0.6 copy-done.6
  36.2 0.0 copy-start.7
  36.2 0.6 copy-done.7
  36.8 0.0 copy-start.8
  36.8 0.6 copy-done.8
  37.4 0.0 copy-start.9
  37.4 0.6 copy-done.9
  38.0 34.9 %local_work.1 = f32[64,20480]{1,0:T(8,128)} custom-call(f32[4]{0:T(128)} %pad_maximum_fusion.params, bf16[64,20480]{1,0:T(8,128)(2,1)} %fine.3, bf16[64,1280]{1,0:T(8,128)(2,1)} %copy-done.2, bf16[64,1280]{1,0:T(8,128)(2,1)} %copy-done.3, bf16[16,5120]{1,0:T(8,128)(2,1)} %copy-done.4, bf16[16,5120]{1,0:T(8,128)(2,1)} %copy-done.5, ...), custom_call_target="tpu_custom_call" | custom-call | tf_op jit(solution)/shard_map/local_work/pallas_call | solution.py:420
Async XLA Ops:
  2.6 1.7 %copy-start = (bf16[64,20480]{1,0:T(8,128)(2,1)S(1)}, bf16[64,20480]{1,0:T(8,128)(2,1)}, u32[]{:S(2)}) copy-start(bf16[64,20480]{1,0:T(8,128)(2,1)} %fine.3) | copy-start | bytes 7864324
  32.1 0.8 %copy-start.1 = (bf16[22,32,384]{2,1,0:T(8,128)(2,1)}, bf16[22,32,384]{2,1,0:T(8,128)(2,1)S(1)}, u32[]{:S(2)}) copy-start(bf16[22,32,384]{2,1,0:T(8,128)(2,1)S(1)} %get-tuple-element.22.patch) | copy-start | bytes 1622020
  32.9 0.7 copy-start.2
  33.6 0.7 copy-start.3
  34.3 0.7 copy-start.4
  34.9 0.7 copy-start.5
  35.6 0.6 copy-start.6
  36.2 0.6 copy-start.7
  36.8 0.6 copy-start.8
  37.4 0.6 copy-start.9
where the time goes:
time: 73.2 us; the launch traced here: 73.1 us
  Pallas kernels  62.7 us (86%)
  local copies, waits for them, and re-layouts  8.75 us (12%)
  between operations  1.02 us (1%)
    pallas_call x1, Pallas kernels, local_work(): pl.pallas_call(functools.partial(local_kernel, where), out_shape=jax.Shap...  34.9 us
    pallas_call x1, Pallas kernels, exchange(): pl.pallas_call(exchange_kernel, out_shape=(side, side, flat, flat, corner...  27.8 us
    unnamed x21, local copies, waits for them, and re-layouts  8.69 us

commit v1 on v0

v1 whole, which is shorter than its diff:
```python
import functools
import math

import jax
import jax.numpy as jnp
from jax import lax
from jax.experimental import pallas as pl
from jax.experimental.pallas import tpu as pltpu
from jax.sharding import PartitionSpec as P

STEPS = 50
C = 320
ROWS = 8
COLS = 16
PAIR = 2 * C
TALL = 64
PAIRS = 32
CHUNK = 8
CELLS = CHUNK * TALL
SHIFTS = (-4, -1, 0, 1, 4)
KEYS = 6144
PITCH = 20
MESH = pl.DeviceIdType.MESH
VMEM_LIMIT = 60 * 1024 * 1024


def silu(x):
    return x / (1.0 + jnp.exp(-x))


def tap_pieces(parity):
    out = []
    for s in (1, 2, 3):
        if parity == 0:
            out += [(s, -1, 2, 3), (s, 0, 0, 5)]
        else:
            out += [(s, 0, 0, 5), (s, 1, 0, 3)]
    first = 0 if parity == 0 else 2
    for s in (0, 2, 4):
        for off in (-2, 0, 2):
            if s == 2 and off == 0:
                continue
            out.append((s, off, first, 3))
    return out


def whole_kernel(
    timestep, fine, coarse_row, coarse_first, coarse_second, local_weight, dilated_weight, out,
    raw, shifted, taps_raw, taps, first_taps, second_taps, hal_top, hal_low, packed, edges, corners, lifted,
    row_in, window_row, patch_in, grid_act, grid_raw, cells1, cells2, cells3, keys1, keys2, turned, blocks, acc, staged,
    in_sem, w_sem, out_sem, send_sem, recv_sem, patch_send, patch_recv,
):
    f32, bf = jnp.float32, jnp.bfloat16
    r = lax.axis_index("row")
    c = lax.axis_index("col")
    above = r > 0
    below = r < ROWS - 1
    down = jnp.logical_and(below, c >= 13)
    up = jnp.logical_and(above, c < 3)

    def present(dr, dc):
        ok = None
        for cond, need in ((above, dr < 0), (below, dr > 0), (c > 0, dc < 0), (c < COLS - 1, dc > 0)):
            if need:
                ok = cond if ok is None else jnp.logical_and(ok, cond)
        return ok

    barrier = pltpu.get_barrier_semaphore()

    def greet(dev):
        pl.semaphore_signal(barrier, inc=1, device_id=dev, device_id_type=MESH)

    def greet_row(step, _):
        greet((r, lax.rem(c + step, COLS)))
        return 0

    lax.fori_loop(1, COLS, greet_row, 0)
    diagonal = ((-1, -1), (-1, 0), (-1, 1), (1, -1), (1, 0), (1, 1))
    expected = COLS - 1 + jnp.where(down, COLS, 0) + jnp.where(up, COLS, 0)
    for step in diagonal:
        @pl.when(present(*step))
        def _(step=step):
            greet((r + step[0], c + step[1]))
        expected = expected + jnp.where(present(*step), 1, 0)
    for k in range(3):
        @pl.when(above)
        def _(k=k):
            greet((r - 1, 13 + k))

        @pl.when(below)
        def _(k=k):
            greet((r + 1, k))

    row_load = pltpu.make_async_copy(coarse_row, row_in, in_sem.at[PAIRS])
    row_load.start()
    loads = []
    for p in range(PAIRS):
        cp = pltpu.make_async_copy(fine.at[:, pl.ds(PAIR * p, PAIR)], raw.at[p + 2], in_sem.at[p])
        cp.start()
        loads.append(cp)
    w_loads = []
    for k, ref in enumerate((dilated_weight, local_weight, coarse_first, coarse_second)):
        cp = pltpu.make_async_copy(ref, taps_raw.at[k], w_sem.at[k])
        cp.start()
        w_loads.append(cp)

    side_zero = jnp.zeros((2, TALL, PAIR), bf)

    @pl.when(c == 0)
    def _():
        raw[0:2] = side_zero
        corners[0] = jnp.zeros((2, 16, PAIR), bf)
        corners[2] = jnp.zeros((2, 16, PAIR), bf)

    @pl.when(c == COLS - 1)
    def _():
        raw[34:36] = side_zero
        corners[1] = jnp.zeros((2, 16, PAIR), bf)
        corners[3] = jnp.zeros((2, 16, PAIR), bf)

    @pl.when(jnp.logical_not(above))
    def _():
        edges[0] = jnp.zeros((8, 16, PAIR), bf)
        corners[0] = jnp.zeros((2, 16, PAIR), bf)
        corners[1] = jnp.zeros((2, 16, PAIR), bf)
        patch_in[0:3] = jnp.zeros((3, 32, 384), bf)

    @pl.when(jnp.logical_not(below))
    def _():
        edges[1] = jnp.zeros((8, 16, PAIR), bf)
        corners[2] = jnp.zeros((2, 16, PAIR), bf)
        corners[3] = jnp.zeros((2, 16, PAIR), bf)
        patch_in[19:22] = jnp.zeros((3, 32, 384), bf)

    row_load.wait()
    turned_row = jnp.concatenate([row_in[...].astype(f32), jnp.zeros((64, 256), f32)], axis=0)
    acc[0:256, 0:384] = jnp.transpose(turned_row)
    window_row[...] = jnp.concatenate(
        [jnp.zeros((4, 384), f32), acc[0:256, 0:384], jnp.zeros((28, 384), f32)], axis=0).astype(bf)
    for cp in loads:
        cp.wait()
    for slot, first in ((0, 0), (1, 12)):
        for q in range(8):
            rows = []
            for g in range(4):
                base = 0 if slot == 0 else 48
                rows.append(raw[2 + 8 * g + q, base : base + 16, :].astype(f32)[first : first + 4])
            packed[slot, q] = jnp.concatenate(rows, axis=0).astype(bf)
    pl.semaphore_wait(barrier, expected)

    last = pl.ds(32, 2)
    head = pl.ds(2, 2)
    upper, lower = pl.ds(0, 16), pl.ds(48, 16)
    sides = (
        ((0, 1), raw.at[last], raw.at[pl.ds(0, 2)]),
        ((0, -1), raw.at[head], raw.at[pl.ds(34, 2)]),
        ((1, 0), packed.at[1], edges.at[0]),
        ((-1, 0), packed.at[0], edges.at[1]),
        ((1, 1), raw.at[last, lower], corners.at[0]),
        ((1, -1), raw.at[head, lower], corners.at[1]),
        ((-1, 1), raw.at[last, upper], corners.at[2]),
        ((-1, -1), raw.at[head, upper], corners.at[3]),
    )

    def side_copy(k):
        step, src, dst = sides[k]
        return pltpu.make_async_remote_copy(
            src_ref=src, dst_ref=dst, send_sem=send_sem.at[k], recv_sem=recv_sem.at[k],
            device_id=(r + step[0], c + step[1]), device_id_type=MESH)

    for k in range(8):
        @pl.when(present(*sides[k][0]))
        def _(k=k):
            side_copy(k).start()

    def window(target):
        return window_row.at[pl.ds(pl.multiple_of(16 * target, 16), 32), :]

    def patch_copy(dev_r, dev_c, k, slot):
        return pltpu.make_async_remote_copy(
            src_ref=window(dev_c), dst_ref=patch_in.at[k], send_sem=patch_send.at[slot, dev_c],
            recv_sem=patch_recv.at[k], device_id=(dev_r, dev_c), device_id_type=MESH)

    own = pltpu.make_async_copy(window(c), patch_in.at[c + 3], patch_recv.at[c + 3])
    own.start()

    def send_row(step, _):
        patch_copy(r, lax.rem(c + step, COLS), c + 3, 0).start()
        return 0

    lax.fori_loop(1, COLS, send_row, 0)

    @pl.when(down)
    def _():
        def one(step, _):
            patch_copy(r + 1, lax.rem(c + step, COLS), c - 13, 1).start()
            return 0
        lax.fori_loop(0, COLS, one, 0)

    @pl.when(up)
    def _():
        def one(step, _):
            patch_copy(r - 1, lax.rem(c + step, COLS), c + 19, 1).start()
            return 0
        lax.fori_loop(0, COLS, one, 0)

    angle = jnp.full((8, 128), timestep[0].astype(f32) * (math.pi / STEPS), f32)
    mix_all = (1.0 + jnp.cos(angle)) * 0.5
    skip_all = mix_all * mix_all * mix_all
    gain_all = (1.0 - skip_all) * mix_all
    one_of = lambda v: v[0:1, 0:1]
    ratio, lift = one_of((1.0 - mix_all) / mix_all), one_of(skip_all / gain_all)
    keep, gain = one_of(1.0 - skip_all), one_of(gain_all)

    for cp in w_loads:
        cp.wait()
    gap = jnp.zeros((C, 64), bf)
    dilated = lambda a, b: taps_raw[0, 3 * a + b]
    local = lambda a, b: (ratio * taps_raw[1, 3 * a + b].astype(f32)).astype(bf)
    for par in range(2):
        at = 0
        for a in range(3):
            row = []
            for b in range(3):
                if a == 1 and b == 1:
                    row.append((dilated(1, 1).astype(f32) + ratio * taps_raw[1, 4].astype(f32)).astype(bf))
                else:
                    row.append(local(a, b))
            row = [gap] + row if par == 0 else row + [gap]
            taps[par, :, at : at + 1024] = jnp.concatenate(row, axis=1)
            at += 1024
        for a in range(3):
            for b in range(3):
                if a == 1 and b == 1:
                    continue
                w = dilated(a, b)
                taps[par, :, at : at + 384] = jnp.concatenate([w, gap] if par == 0 else [gap, w], axis=1)
                at += 384
    for k in range(9):
        first_taps[:, 384 * k : 384 * k + 384] = jnp.concatenate([taps_raw[2, k], gap], axis=1)
        second_taps[:, 384 * k : 384 * k + 384] = jnp.concatenate([taps_raw[3, k], gap], axis=1)
    eye = lax.broadcasted_iota(jnp.int32, (C, 384), 0) == lax.broadcasted_iota(jnp.int32, (C, 384), 1)
    second_taps[:, 3456:3840] = eye.astype(f32).astype(bf)

    for k in range(8):
        step, src, dst = sides[k]
        @pl.when(present(-step[0], -step[1]))
        def _(k=k):
            side_copy(k).wait_recv()

    hal_top[...] = jnp.zeros_like(hal_top)
    hal_low[...] = jnp.zeros_like(hal_low)
    for slot, ref, base in ((0, hal_top, 4), (1, hal_low, 0)):
        for q in range(8):
            block = edges[slot, q].astype(f32)
            for g in range(4):
                ref[2 + 8 * g + q, base : base + 4, :] = block[4 * g : 4 * g + 4]
    for p in range(2):
        hal_top[p, 4:8, :] = corners[0, p].astype(f32)[12:16]
        hal_top[34 + p, 4:8, :] = corners[1, p].astype(f32)[12:16]
        hal_low[p, 0:4, :] = corners[2, p].astype(f32)[0:4]
        hal_low[34 + p, 0:4, :] = corners[3, p].astype(f32)[0:4]

    def prepare(p, _):
        lifted[0:8, :] = silu(hal_top[p])
        lifted[8:72, :] = silu(raw[p].astype(f32))
        lifted[72:80, :] = silu(hal_low[p])
        for k, s in enumerate(SHIFTS):
            shifted[k, p] = lifted[8 + s : 72 + s, :].astype(bf)
        return 0

    lax.fori_loop(0, PAIRS + 4, prepare, 0)

    own.wait()

    def got_row(step, _):
        k = lax.rem(c + step, COLS) + 3
        pltpu.make_async_copy(window_row.at[pl.ds(0, 32), :], patch_in.at[k], patch_recv.at[k]).wait()
        return 0

    lax.fori_loop(1, COLS, got_row, 0)
    for k in range(3):
        for cond, slot in ((above, k), (below, 19 + k)):
            @pl.when(cond)
            def _(slot=slot):
                pltpu.make_async_copy(window_row.at[pl.ds(0, 32), :], patch_in.at[slot], patch_recv.at[slot]).wait()

    values = patch_in[...].astype(f32).reshape(22 * 32, 384)
    for t in range(3):
        part = values[:, 128 * t : 128 * t + 128]
        grid_raw[t] = part
        grid_act[t] = silu(part)
    cells1[...] = jnp.zeros_like(cells1)
    cells2[...] = jnp.zeros_like(cells2)
    cells3[...] = jnp.zeros_like(cells3)
    for t in range(3):
        lanes = slice(128 * t, 128 * t + 128)
        for m in range(22):
            cells1[24 * m : 24 * m + 22, lanes] = grid_act[t, pl.ds(m + 1, 22, stride=32), :]
        for m in range(18):
            cells3[PITCH * m : PITCH * m + PITCH, lanes] = grid_raw[t, pl.ds(64 + m + 3, PITCH, stride=32), :]
    for a in range(3):
        for b in range(3):
            k = 3 * a + b
            first = 24 * b + a
            keys1[:, 384 * k : 384 * k + 384] = cells1[first : first + 512, :].astype(bf)
    contract = (((1,), (1,)), ((), ()))
    hidden = lax.dot_general(first_taps[...], keys1[...], contract, preferred_element_type=f32)
    hidden = jnp.concatenate([silu(hidden), jnp.zeros((64, 512), f32)], axis=0)
    turned[...] = jnp.transpose(hidden)
    field_row = lax.broadcasted_iota(jnp.int32, (PITCH, 384), 0) + (16 * r - 2)
    row_ok = jnp.logical_and(field_row >= 0, field_row < 128)
    for m in range(20):
        col = 16 * c - 2 + m
        ok = jnp.logical_and(row_ok, jnp.logical_and(col >= 0, col < 256))
        cells2[PITCH * m : PITCH * m + PITCH, :] = jnp.where(ok, turned[24 * m : 24 * m + PITCH, :], 0.0)
    for a in range(3):
        for b in range(3):
            k = 3 * a + b
            first = PITCH * b + a
            keys2[:, 384 * k : 384 * k + 384] = cells2[first : first + 384, :].astype(bf)
    keys2[:, 3456:3840] = cells3[...].astype(bf)
    coarse = lift * lax.dot_general(second_taps[...], keys2[...], contract, preferred_element_type=f32)
    for q in range(4):
        part = coarse if q == 0 else pltpu.roll(coarse, 384 - 80 * q, axis=1)
        part = part[:, 0:128]
        high = part.astype(bf)
        blocks[q, :, 0:128] = high
        blocks[q, :, 128:256] = (part - high.astype(f32)).astype(bf)

    lane = lax.broadcasted_iota(jnp.int32, (TALL, 128), 1)
    group = jnp.zeros((TALL, 128), jnp.int32)
    for t in range(1, 7):
        group = group + (lane >= PITCH * t).astype(jnp.int32)
    lane_row = (lane - PITCH * group + (16 * r - 1)).astype(f32)
    lane_col = (group + (16 * c - 1)).astype(f32)
    fine_row = (lax.broadcasted_iota(jnp.int32, (TALL, 128), 0) + 64 * r).astype(f32)
    where_row = jnp.clip((fine_row + 0.5) * 0.25 - 0.5, 0.0, 127.0)
    row_share = jnp.maximum(1.0 - jnp.abs(where_row - lane_row), 0.0)
    base_col = (jnp.zeros((TALL, 128), jnp.int32) + 64 * c).astype(f32)

    def shares(q, par):
        out = []
        for pp in range(CHUNK):
            spot = jnp.clip((base_col + (16 * q + 2 * pp + par + 0.5)) * 0.25 - 0.5, 0.0, 255.0)
            part = row_share * jnp.maximum(1.0 - jnp.abs(spot - (lane_col + 4 * q)), 0.0)
            out.append(jnp.concatenate([part, part], axis=1).astype(bf))
        return jnp.concatenate(out, axis=0)

    pending = [None, None]
    for q in range(4):
        for par in range(2):
            pieces = []
            for s, off, tile, n in tap_pieces(par):
                first = 2 + CHUNK * q + off
                part = shifted[s, first : first + CHUNK, :, 128 * tile : 128 * (tile + n)]
                pieces.append(part.reshape(CELLS, 128 * n))
            pieces.append(shares(q, par))
            rhs = jnp.concatenate(pieces, axis=1)
            lhs = jnp.concatenate([taps[par], blocks[q]], axis=1)
            acc[C * par : C * par + C, :] = lax.dot_general(lhs, rhs, contract, preferred_element_type=f32)
        slot = q % 2
        if pending[slot] is not None:
            pending[slot].wait()
        for u in range(CHUNK // 2):
            block = jnp.transpose(acc[:, 128 * u : 128 * u + 128])
            for v in range(2):
                pp = 2 * u + v
                cells = raw[2 + CHUNK * q + pp].astype(f32)
                staged[slot, :, PAIR * pp : PAIR * (pp + 1)] = keep * cells + gain * block[64 * v : 64 * v + 64]
        cp = pltpu.make_async_copy(staged.at[slot], out.at[:, pl.ds(5120 * q, 5120)], out_sem.at[slot])
        cp.start()
        pending[slot] = cp
    for cp in pending:
        cp.wait()

    for k in range(8):
        @pl.when(present(*sides[k][0]))
        def _(k=k):
            side_copy(k).wait_send()

    def sent_row(step, _):
        patch_copy(r, lax.rem(c + step, COLS), c + 3, 0).wait_send()
        return 0

    lax.fori_loop(1, COLS, sent_row, 0)

    @pl.when(down)
    def _():
        def one(step, _):
            patch_copy(r + 1, lax.rem(c + step, COLS), c - 13, 1).wait_send()
            return 0
        lax.fori_loop(0, COLS, one, 0)

    @pl.when(up)
    def _():
        def one(step, _):
            patch_copy(r - 1, lax.rem(c + step, COLS), c + 19, 1).wait_send()
            return 0
        lax.fori_loop(0, COLS, one, 0)


def whole(*arrays):
    f32, bf = jnp.float32, jnp.bfloat16
    any_spec = pl.BlockSpec(memory_space=pl.ANY)
    return pl.pallas_call(
        whole_kernel,
        out_shape=jax.ShapeDtypeStruct((64, 20480), f32),
        in_specs=[pl.BlockSpec(memory_space=pltpu.SMEM)] + [any_spec] * 6,
        out_specs=any_spec,
        scratch_shapes=[
            pltpu.VMEM((36, 64, 640), bf),
            pltpu.VMEM((5, 36, 64, 640), bf),
            pltpu.VMEM((4, 9, C, C), bf),
            pltpu.VMEM((2, C, KEYS), bf),
            pltpu.VMEM((C, 3456), bf),
            pltpu.VMEM((C, 3840), bf),
            pltpu.VMEM((36, 8, 640), f32),
            pltpu.VMEM((36, 8, 640), f32),
            pltpu.VMEM((2, 8, 16, 640), bf),
            pltpu.VMEM((2, 8, 16, 640), bf),
            pltpu.VMEM((4, 2, 16, 640), bf),
            pltpu.VMEM((80, 640), f32),
            pltpu.VMEM((C, 256), bf),
            pltpu.VMEM((288, 384), bf),
            pltpu.VMEM((22, 32, 384), bf),
            pltpu.VMEM((3, 704, 128), f32),
            pltpu.VMEM((3, 704, 128), f32),
            pltpu.VMEM((568, 384), f32),
            pltpu.VMEM((432, 384), f32),
            pltpu.VMEM((384, 384), f32),
            pltpu.VMEM((512, 3456), bf),
            pltpu.VMEM((384, 3840), bf),
            pltpu.VMEM((512, 384), f32),
            pltpu.VMEM((4, C, 256), bf),
            pltpu.VMEM((PAIR, CELLS), f32),
            pltpu.VMEM((2, 64, 5120), f32),
            pltpu.SemaphoreType.DMA((PAIRS + 1,)),
            pltpu.SemaphoreType.DMA((4,)),
            pltpu.SemaphoreType.DMA((2,)),
            pltpu.SemaphoreType.DMA((8,)),
            pltpu.SemaphoreType.DMA((8,)),
            pltpu.SemaphoreType.DMA((2, COLS)),
            pltpu.SemaphoreType.DMA((22,)),
        ],
        compiler_params=pltpu.CompilerParams(collective_id=0, has_side_effects=True, vmem_limit_bytes=VMEM_LIMIT),
        name="whole",
    )(*arrays)


def on_device(coarse_latent, fine_latent, timestep, coarse_first, coarse_second, local_weight, dilated_weight):
    flat = lambda w: w.reshape(9, C, C)
    return whole(
        timestep, fine_latent, coarse_latent.reshape(C, 256),
        flat(coarse_first), flat(coarse_second), flat(local_weight), flat(dilated_weight))


def solution(mesh):
    placed = (P(None, ("row", "col"), None), P("row", "col"), P(), P(), P(), P(), P())
    return jax.shard_map(
        on_device, mesh=mesh, in_specs=placed, out_specs=P("row", "col"), check_vma=False
    )
```

time: 73.2 us -> 61.3 us (0.84)
  Pallas kernels: 62.7 us -> 55.3 us
  local copies, waits for them, and re-layouts: 8.75 us -> 5.22 us
    pallas_call x2 -> x1, Pallas kernels: 62.7 us -> 55.3 us  [whole(): pl.pallas_call(whole_kernel, out_shape=jax.ShapeDtypeStruct((64, 20480),...]
    unnamed x21 -> x1, local copies, waits for them, and re-layouts: 8.69 us -> 5.22 us
where the time goes in v1:
time: 61.3 us; the launch traced here: 61.2 us
  Pallas kernels  55.3 us (90%)
  local copies, waits for them, and re-layouts  5.22 us (9%)
  between operations  0.66 us (1%)
    pallas_call x1, Pallas kernels, whole(): pl.pallas_call(whole_kernel, out_shape=jax.ShapeDtypeStruct((64, 20480),...  55.3 us
    unnamed x1, local copies, waits for them, and re-layouts  5.22 us

profile of v1, /device:TPU:1, one launch (start us, length us, event | category | flops | bytes accessed | tf_op | source)
XLA Modules:
  0.0 61.2 jit_solution(15478963065848460786)
XLA Ops:
  0.7 55.3 %whole.1 = f32[64,20480]{1,0:T(8,128)} custom-call(s32[1]{0:T(128)S(6)} %copy.9.timestep, bf16[64,20480]{1,0:T(8,128)(2,1)} %fine.1, bf16[320,256]{1,0:T(8,128)(2,1)} %bitcast.9, bf16[9,320,320]{2,1,0:T(8,128)(2,1)} %bitcast.5, bf16[9,320,320]{2,1,0:T(8,128)(2,1)} %bitcast.6, bf16[9,320,320]{2,1,0:T(8,128)(2,1)} %bitcast.7, bf16[9,320,320]{2,1,0:T(8,128)(2,1)} %bitcast.8), custom_call_target="tpu_custom_call" | custom-call | tf_op jit(solution)/shard_map/whole/pallas_call | solution.py:406
  55.9 5.2 %copy.10 = f32[64,20480]{1,0:T(8,128)} copy(f32[64,20480]{1,0:T(8,128)} %whole.1) | data formatting | bytes 10485760

commit v2 on v1

v2 whole, which is shorter than its diff:
```python
import functools
import math

import jax
import jax.numpy as jnp
from jax import lax
from jax.experimental import pallas as pl
from jax.experimental.pallas import tpu as pltpu
from jax.sharding import PartitionSpec as P

STEPS = 50
C = 320
ROWS = 8
COLS = 16
PAIR = 2 * C
TALL = 64
PAIRS = 32
CHUNK = 16
CELLS = CHUNK * 32
SHIFTS = (-4, -1, 0, 1, 4)
KEYS = 6144
PITCH = 20
MESH = pl.DeviceIdType.MESH
VMEM_LIMIT = 60 * 1024 * 1024


def silu(x):
    return x / (1.0 + jnp.exp(-x))


def tap_pieces(parity):
    out = []
    for s in (1, 2, 3):
        if parity == 0:
            out += [(s, -1, 2, 3), (s, 0, 0, 5)]
        else:
            out += [(s, 0, 0, 5), (s, 1, 0, 3)]
    first = 0 if parity == 0 else 2
    for s in (0, 2, 4):
        for off in (-2, 0, 2):
            if s == 2 and off == 0:
                continue
            out.append((s, off, first, 3))
    return out


def whole_kernel(
    timestep, fine, coarse_row, coarse_first, coarse_second, local_weight, dilated_weight, out,
    raw, shifted, taps_raw, taps, packed, edges, corner_out, corners, row_in, window_row, patch_in, blocks, acc, staged,
    in_sem, w_sem, out_sem, send_sem, recv_sem, patch_send, patch_recv,
):
    f32, bf = jnp.float32, jnp.bfloat16
    r = lax.axis_index("row")
    c = lax.axis_index("col")
    above = r > 0
    below = r < ROWS - 1
    down = jnp.logical_and(below, c >= 13)
    up = jnp.logical_and(above, c < 3)

    def present(dr, dc):
        ok = None
        for cond, need in ((above, dr < 0), (below, dr > 0), (c > 0, dc < 0), (c < COLS - 1, dc > 0)):
            if need:
                ok = cond if ok is None else jnp.logical_and(ok, cond)
        return ok

    barrier = pltpu.get_barrier_semaphore()

    def greet(dev):
        pl.semaphore_signal(barrier, inc=1, device_id=dev, device_id_type=MESH)

    def greet_row(step, _):
        greet((r, lax.rem(c + step, COLS)))
        return 0

    lax.fori_loop(1, COLS, greet_row, 0)
    diagonal = ((-1, -1), (-1, 0), (-1, 1), (1, -1), (1, 0), (1, 1))
    expected = COLS - 1 + jnp.where(down, COLS, 0) + jnp.where(up, COLS, 0)
    for step in diagonal:
        @pl.when(present(*step))
        def _(step=step):
            greet((r + step[0], c + step[1]))
        expected = expected + jnp.where(present(*step), 1, 0)
    for k in range(3):
        @pl.when(above)
        def _(k=k):
            greet((r - 1, 13 + k))

        @pl.when(below)
        def _(k=k):
            greet((r + 1, k))

    row_load = pltpu.make_async_copy(coarse_row, row_in, in_sem.at[PAIRS])
    row_load.start()
    loads = []
    for p in range(PAIRS):
        cp = pltpu.make_async_copy(fine.at[:, pl.ds(PAIR * p, PAIR)], raw.at[p + 2], in_sem.at[p])
        cp.start()
        loads.append(cp)
    w_loads = []
    for k, ref in enumerate((dilated_weight, local_weight, coarse_first, coarse_second)):
        cp = pltpu.make_async_copy(ref, taps_raw.at[k], w_sem.at[k])
        cp.start()
        w_loads.append(cp)

    side_zero = jnp.zeros((2, TALL, PAIR), bf)

    @pl.when(c == 0)
    def _():
        raw[0:2] = side_zero
        corners[0] = jnp.zeros((16, PAIR), bf)
        corners[2] = jnp.zeros((16, PAIR), bf)

    @pl.when(c == COLS - 1)
    def _():
        raw[34:36] = side_zero
        corners[1] = jnp.zeros((16, PAIR), bf)
        corners[3] = jnp.zeros((16, PAIR), bf)

    @pl.when(jnp.logical_not(above))
    def _():
        edges[0] = jnp.zeros((8, 16, PAIR), bf)
        corners[0] = jnp.zeros((16, PAIR), bf)
        corners[1] = jnp.zeros((16, PAIR), bf)
        patch_in[0:3] = jnp.zeros((3, 32, 384), bf)

    @pl.when(jnp.logical_not(below))
    def _():
        edges[1] = jnp.zeros((8, 16, PAIR), bf)
        corners[2] = jnp.zeros((16, PAIR), bf)
        corners[3] = jnp.zeros((16, PAIR), bf)
        patch_in[19:22] = jnp.zeros((3, 32, 384), bf)

    row_load.wait()
    turned_row = jnp.concatenate([row_in[...].astype(f32), jnp.zeros((64, 256), f32)], axis=0)
    window_row[...] = jnp.concatenate(
        [jnp.zeros((4, 384), f32), jnp.transpose(turned_row), jnp.zeros((28, 384), f32)], axis=0).astype(bf)
    for cp in loads:
        cp.wait()
    for slot, base, first in ((0, 0, 0), (1, 48, 12)):
        tops = {}
        for p in range(PAIRS):
            tops[p] = raw[2 + p, base : base + 16, :].astype(f32)[first : first + 4]
        for q in range(8):
            packed[slot, q] = jnp.concatenate([tops[8 * g + q] for g in range(4)], axis=0).astype(bf)
        for k, p in ((0, 30), (1, 0)):
            spot = k if slot == 1 else 2 + k
            corner_out[spot] = jnp.concatenate([tops[p], tops[p + 1], jnp.zeros((8, PAIR), f32)], axis=0).astype(bf)
    pl.semaphore_wait(barrier, expected)

    last = pl.ds(32, 2)
    head = pl.ds(2, 2)
    sides = (
        ((0, 1), raw.at[last], raw.at[pl.ds(0, 2)]),
        ((0, -1), raw.at[head], raw.at[pl.ds(34, 2)]),
        ((1, 0), packed.at[1], edges.at[0]),
        ((-1, 0), packed.at[0], edges.at[1]),
        ((1, 1), corner_out.at[0], corners.at[0]),
        ((1, -1), corner_out.at[1], corners.at[1]),
        ((-1, 1), corner_out.at[2], corners.at[2]),
        ((-1, -1), corner_out.at[3], corners.at[3]),
    )

    def side_copy(k):
        step, src, dst = sides[k]
        return pltpu.make_async_remote_copy(
            src_ref=src, dst_ref=dst, send_sem=send_sem.at[k], recv_sem=recv_sem.at[k],
            device_id=(r + step[0], c + step[1]), device_id_type=MESH)

    for k in range(8):
        @pl.when(present(*sides[k][0]))
        def _(k=k):
            side_copy(k).start()

    def window(target):
        return window_row.at[pl.ds(pl.multiple_of(16 * target, 16), 32), :]

    def patch_copy(dev_r, dev_c, k, slot):
        return pltpu.make_async_remote_copy(
            src_ref=window(dev_c), dst_ref=patch_in.at[k], send_sem=patch_send.at[slot, dev_c],
            recv_sem=patch_recv.at[k], device_id=(dev_r, dev_c), device_id_type=MESH)

    own = pltpu.make_async_copy(window(c), patch_in.at[c + 3], patch_recv.at[c + 3])
    own.start()

    def send_row(step, _):
        patch_copy(r, lax.rem(c + step, COLS), c + 3, 0).start()
        return 0

    lax.fori_loop(1, COLS, send_row, 0)

    @pl.when(down)
    def _():
        def one(step, _):
            patch_copy(r + 1, lax.rem(c + step, COLS), c - 13, 1).start()
            return 0
        lax.fori_loop(0, COLS, one, 0)

    @pl.when(up)
    def _():
        def one(step, _):
            patch_copy(r - 1, lax.rem(c + step, COLS), c + 19, 1).start()
            return 0
        lax.fori_loop(0, COLS, one, 0)

    angle = jnp.full((8, 128), timestep[0].astype(f32) * (math.pi / STEPS), f32)
    mix_all = (1.0 + jnp.cos(angle)) * 0.5
    skip_all = mix_all * mix_all * mix_all
    gain_all = (1.0 - skip_all) * mix_all
    one_of = lambda v: v[0:1, 0:1]
    ratio, lift = one_of((1.0 - mix_all) / mix_all), one_of(skip_all / gain_all)
    keep, gain = one_of(1.0 - skip_all), one_of(gain_all)

    for cp in w_loads:
        cp.wait()
    gap = jnp.zeros((C, 64), bf)
    dilated = lambda a, b: taps_raw[0, 3 * a + b]
    local = lambda a, b: (ratio * taps_raw[1, 3 * a + b].astype(f32)).astype(bf)
    for par in range(2):
        at = 0
        for a in range(3):
            row = []
            for b in range(3):
                if a == 1 and b == 1:
                    row.append((dilated(1, 1).astype(f32) + ratio * taps_raw[1, 4].astype(f32)).astype(bf))
                else:
                    row.append(local(a, b))
            row = [gap] + row if par == 0 else row + [gap]
            taps[par, :, at : at + 1024] = jnp.concatenate(row, axis=1)
            at += 1024
        for a in range(3):
            for b in range(3):
                if a == 1 and b == 1:
                    continue
                w = dilated(a, b)
                taps[par, :, at : at + 384] = jnp.concatenate([w, gap] if par == 0 else [gap, w], axis=1)
                at += 384
    contract = (((1,), (1,)), ((), ()))

    lane = lax.broadcasted_iota(jnp.int32, (TALL, 256), 1)
    group = jnp.zeros((TALL, 256), jnp.int32)
    for t in range(1, 13):
        group = group + (lane >= PITCH * t).astype(jnp.int32)
    lane_row = (lane - PITCH * group + (16 * r - 1)).astype(f32)
    lane_col = (group[0:8] + (16 * c - 1)).astype(f32)
    fine_row = (lax.broadcasted_iota(jnp.int32, (TALL, 256), 0) + 64 * r).astype(f32)
    where_row = jnp.clip((fine_row + 0.5) * 0.25 - 0.5, 0.0, 127.0)
    row_share = jnp.maximum(1.0 - jnp.abs(where_row - lane_row), 0.0)
    base_col = (jnp.zeros((8, 256), jnp.int32) + 64 * c).astype(f32)
    inner = row_share[16:48].reshape(4, 8, 256)
    outer = jnp.concatenate([row_share[0:16], row_share[48:64]], axis=0).reshape(4, 8, 256)

    def shares(h, par, rim):
        out = []
        for pp in range(CHUNK):
            spot = jnp.clip((base_col + (32 * h + 2 * pp + par + 0.5)) * 0.25 - 0.5, 0.0, 255.0)
            col_share = jnp.maximum(1.0 - jnp.abs(spot - (lane_col + 8 * h)), 0.0)
            part = ((outer if rim else inner) * col_share[None]).reshape(32, 256)
            out.append(jnp.concatenate([part, part], axis=1).astype(bf))
        return jnp.concatenate(out, axis=0)

    def keys_of(h, par, rim):
        pieces = []
        for s, off, tile, n in tap_pieces(par):
            cells = pl.ds(2 + CHUNK * h + off, CHUNK)
            lanes = slice(128 * tile, 128 * (tile + n))
            if rim:
                part = jnp.concatenate([shifted[s, cells, 0:16, lanes], shifted[s, cells, 48:64, lanes]], axis=1)
            else:
                part = shifted[s, cells, 16:48, lanes]
            pieces.append(part.reshape(CELLS, 128 * n))
        return pieces

    def arrived(k):
        step = sides[k][0]

        @pl.when(present(-step[0], -step[1]))
        def _():
            side_copy(k).wait_recv()

    def fine_work(lifted):
        def first_part(p, _):
            values = silu(raw[p].astype(f32))
            lifted[p, 8:72, :] = values
            shifted[2, p] = values.astype(bf)
            for k in (0, 1, 3, 4):
                s = SHIFTS[k]
                shifted[k, p, 16:48, :] = lifted[p, 24 + s : 56 + s, :].astype(bf)
            return 0

        lax.fori_loop(2, PAIRS + 2, first_part, 0)
        arrived(0)
        arrived(1)
        for p in (0, 1, 34, 35):
            first_part(p, 0)
        for h in range(2):
            for par in range(2):
                rhs = jnp.concatenate(keys_of(h, par, False), axis=1)
                acc[h, C * par : C * par + C, :] = lax.dot_general(taps[par], rhs, contract, preferred_element_type=f32)
        for k in range(2, 8):
            arrived(k)
        for slot, base in ((0, 4), (1, 72)):
            for q in range(8):
                block = silu(edges[slot, q].astype(f32))
                for g in range(4):
                    lifted[2 + 8 * g + q, base : base + 4, :] = block[4 * g : 4 * g + 4]
            for k, first in ((0, 0), (1, 34)):
                block = silu(corners[2 * slot + k].astype(f32))
                for p in range(2):
                    lifted[first + p, base : base + 4, :] = block[4 * p : 4 * p + 4]

        def second_part(p, _):
            for k in (0, 1, 3, 4):
                s = SHIFTS[k]
                shifted[k, p, 0:16, :] = lifted[p, 8 + s : 24 + s, :].astype(bf)
                shifted[k, p, 48:64, :] = lifted[p, 56 + s : 72 + s, :].astype(bf)
            return 0

        lax.fori_loop(0, PAIRS + 4, second_part, 0)

    pl.run_scoped(fine_work, pltpu.VMEM((36, 80, 640), f32))

    own.wait()

    def got_row(step, _):
        k = lax.rem(c + step, COLS) + 3
        pltpu.make_async_copy(window_row.at[pl.ds(0, 32), :], patch_in.at[k], patch_recv.at[k]).wait()
        return 0

    lax.fori_loop(1, COLS, got_row, 0)
    for k in range(3):
        for cond, slot in ((above, k), (below, 19 + k)):
            @pl.when(cond)
            def _(slot=slot):
                pltpu.make_async_copy(window_row.at[pl.ds(0, 32), :], patch_in.at[slot], patch_recv.at[slot]).wait()

    def coarse_work(grid, cells1, cells2, cells3, keys, turned):
        values = patch_in[...].astype(f32).reshape(22 * 32, 384)
        for t in range(3):
            grid[t] = silu(values[:, 128 * t : 128 * t + 128])
        cells1[520:568, :] = jnp.zeros((48, 384), f32)
        cells2[400:432, :] = jnp.zeros((32, 384), f32)
        cells3[360:384, :] = jnp.zeros((24, 384), f32)
        for t in range(3):
            lanes = slice(128 * t, 128 * t + 128)
            for m in range(22):
                cells1[24 * m : 24 * m + 24, lanes] = jnp.concatenate(
                    [grid[t, pl.ds(m + 1, 22, stride=32), :], jnp.zeros((2, 128), f32)], axis=0)
        for t in range(3):
            grid[t] = values[:, 128 * t : 128 * t + 128]
        for t in range(3):
            lanes = slice(128 * t, 128 * t + 128)
            for m in range(18):
                cells3[PITCH * m : PITCH * m + PITCH, lanes] = grid[t, pl.ds(64 + m + 3, PITCH, stride=32), :]
        for a in range(3):
            for b in range(3):
                k = 3 * a + b
                first = 24 * b + a
                keys[:, 384 * k : 384 * k + 384] = cells1[first : first + 512, :].astype(bf)
        widen = lambda w: jnp.concatenate([w, gap], axis=1)
        first_taps = jnp.concatenate([widen(taps_raw[2, k]) for k in range(9)], axis=1)
        hidden = lax.dot_general(first_taps, keys[:, 0:3456], contract, preferred_element_type=f32)
        hidden = jnp.concatenate([silu(hidden), jnp.zeros((64, 512), f32)], axis=0)
        turned[...] = jnp.transpose(hidden)
        field_row = lax.broadcasted_iota(jnp.int32, (PITCH, 384), 0) + (16 * r - 2)
        row_ok = jnp.logical_and(field_row >= 0, field_row < 128)
        for m in range(20):
            col = 16 * c - 2 + m
            ok = jnp.logical_and(row_ok, jnp.logical_and(col >= 0, col < 256))
            cells2[PITCH * m : PITCH * m + PITCH, :] = jnp.where(ok, turned[24 * m : 24 * m + PITCH, :], 0.0)
        for a in range(3):
            for b in range(3):
                k = 3 * a + b
                first = PITCH * b + a
                keys[0:384, 384 * k : 384 * k + 384] = cells2[first : first + 384, :].astype(bf)
        keys[0:384, 3456:3840] = cells3[...].astype(bf)
        eye = lax.broadcasted_iota(jnp.int32, (C, 384), 0) == lax.broadcasted_iota(jnp.int32, (C, 384), 1)
        second_taps = jnp.concatenate([widen(taps_raw[3, k]) for k in range(9)] + [eye.astype(f32).astype(bf)], axis=1)
        coarse = lift * lax.dot_general(second_taps, keys[0:384, :], contract, preferred_element_type=f32)
        for h in range(2):
            part = coarse if h == 0 else pltpu.roll(coarse, 384 - 160, axis=1)
            part = part[:, 0:256]
            high = part.astype(bf)
            blocks[h, :, 0:256] = high
            blocks[h, :, 256:512] = (part - high.astype(f32)).astype(bf)

    pl.run_scoped(
        coarse_work,
        pltpu.VMEM((3, 704, 128), f32),
        pltpu.VMEM((568, 384), f32),
        pltpu.VMEM((432, 384), f32),
        pltpu.VMEM((384, 384), f32),
        pltpu.VMEM((512, 3840), bf),
        pltpu.VMEM((512, 384), f32),
    )

    writes = {}

    def blend(h, rim, source, slot):
        for old in writes.pop(slot, ()):
            old.wait()
        for u in range(CHUNK // 4):
            block = jnp.transpose(acc[source, :, 128 * u : 128 * u + 128])
            for v in range(4):
                pp = 4 * u + v
                cells = raw[2 + CHUNK * h + pp]
                if rim:
                    cells = jnp.concatenate([cells[0:16], cells[48:64]], axis=0)
                else:
                    cells = cells[16:48]
                staged[slot, :, PAIR * pp : PAIR * (pp + 1)] = (
                    keep * cells.astype(f32) + gain * block[32 * v : 32 * v + 32])
        lanes = pl.ds(PAIR * CHUNK * h, PAIR * CHUNK)
        if rim:
            parts = [(pl.ds(0, 16), pl.ds(0, 16)), (pl.ds(16, 16), pl.ds(48, 16))]
        else:
            parts = [(pl.ds(0, 32), pl.ds(16, 32))]
        writes[slot] = []
        for k, (here, there) in enumerate(parts):
            cp = pltpu.make_async_copy(staged.at[slot, here], out.at[there, lanes], out_sem.at[2 * slot + k])
            cp.start()
            writes[slot].append(cp)

    for h in range(2):
        for par in range(2):
            acc[h, C * par : C * par + C, :] += lax.dot_general(
                blocks[h], shares(h, par, False), contract, preferred_element_type=f32)
        target = 2 if h == 0 else 0
        for par in range(2):
            rhs = jnp.concatenate(keys_of(h, par, True) + [shares(h, par, True)], axis=1)
            lhs = jnp.concatenate([taps[par], blocks[h]], axis=1)
            acc[target, C * par : C * par + C, :] = lax.dot_general(lhs, rhs, contract, preferred_element_type=f32)
        if h == 0:
            blend(0, False, 0, 0)
        else:
            blend(1, False, 1, 1)
            blend(0, True, 2, 0)
            blend(1, True, 0, 1)
    for group_of in writes.values():
        for cp in group_of:
            cp.wait()

    for k in range(8):
        @pl.when(present(*sides[k][0]))
        def _(k=k):
            side_copy(k).wait_send()

    def sent_row(step, _):
        patch_copy(r, lax.rem(c + step, COLS), c + 3, 0).wait_send()
        return 0

    lax.fori_loop(1, COLS, sent_row, 0)

    @pl.when(down)
    def _():
        def one(step, _):
            patch_copy(r + 1, lax.rem(c + step, COLS), c - 13, 1).wait_send()
            return 0
        lax.fori_loop(0, COLS, one, 0)

    @pl.when(up)
    def _():
        def one(step, _):
            patch_copy(r - 1, lax.rem(c + step, COLS), c + 19, 1).wait_send()
            return 0
        lax.fori_loop(0, COLS, one, 0)


def whole(*arrays):
    f32, bf = jnp.float32, jnp.bfloat16
    any_spec = pl.BlockSpec(memory_space=pl.ANY)
    return pl.pallas_call(
        whole_kernel,
        out_shape=jax.ShapeDtypeStruct((64, 20480), f32),
        in_specs=[pl.BlockSpec(memory_space=pltpu.SMEM)] + [any_spec] * 6,
        out_specs=any_spec,
        scratch_shapes=[
            pltpu.VMEM((36, 64, 640), bf),
            pltpu.VMEM((5, 36, 64, 640), bf),
            pltpu.VMEM((4, 9, C, C), bf),
            pltpu.VMEM((2, C, KEYS), bf),
            pltpu.VMEM((2, 8, 16, 640), bf),
            pltpu.VMEM((2, 8, 16, 640), bf),
            pltpu.VMEM((4, 16, 640), bf),
            pltpu.VMEM((4, 16, 640), bf),
            pltpu.VMEM((C, 256), bf),
            pltpu.VMEM((288, 384), bf),
            pltpu.VMEM((22, 32, 384), bf),
            pltpu.VMEM((2, C, 512), bf),
            pltpu.VMEM((3, PAIR, CELLS), f32),
            pltpu.VMEM((2, 32, PAIR * CHUNK), f32),
            pltpu.SemaphoreType.DMA((PAIRS + 1,)),
            pltpu.SemaphoreType.DMA((4,)),
            pltpu.SemaphoreType.DMA((4,)),
            pltpu.SemaphoreType.DMA((8,)),
            pltpu.SemaphoreType.DMA((8,)),
            pltpu.SemaphoreType.DMA((2, COLS)),
            pltpu.SemaphoreType.DMA((22,)),
        ],
        compiler_params=pltpu.CompilerParams(collective_id=0, has_side_effects=True, vmem_limit_bytes=VMEM_LIMIT),
        name="whole",
    )(*arrays)


def on_device(coarse_latent, fine_latent, timestep, coarse_first, coarse_second, local_weight, dilated_weight):
    flat = lambda w: w.reshape(9, C, C)
    return whole(
        timestep, fine_latent, coarse_latent.reshape(C, 256),
        flat(coarse_first), flat(coarse_second), flat(local_weight), flat(dilated_weight))


def solution(mesh):
    placed = (P(None, ("row", "col"), None), P("row", "col"), P(), P(), P(), P(), P())
    return jax.shard_map(
        on_device, mesh=mesh, in_specs=placed, out_specs=P("row", "col"), check_vma=False
    )
```

time: 61.3 us -> 49.9 us (0.81)
  Pallas kernels: 55.3 us -> 43.9 us
    pallas_call x1, Pallas kernels: 55.3 us -> 43.9 us  [whole(): pl.pallas_call(whole_kernel, out_shape=jax.ShapeDtypeStruct((64, 20480),...]
where the time goes in v2:
time: 49.9 us; the launch traced here: 49.8 us
  Pallas kernels  43.9 us (88%)
  local copies, waits for them, and re-layouts  5.22 us (10%)
  between operations  0.66 us (1%)
    pallas_call x1, Pallas kernels, whole(): pl.pallas_call(whole_kernel, out_shape=jax.ShapeDtypeStruct((64, 20480),...  43.9 us
    unnamed x1, local copies, waits for them, and re-layouts  5.22 us

profile of v2, /device:TPU:1, one launch (start us, length us, event | category | flops | bytes accessed | tf_op | source)
XLA Modules:
  0.0 49.8 jit_solution(14148262679662592547)
XLA Ops:
  0.7 43.9 %whole.1 = f32[64,20480]{1,0:T(8,128)} custom-call(s32[1]{0:T(128)S(6)} %copy.9.timestep, bf16[64,20480]{1,0:T(8,128)(2,1)} %fine.1, bf16[320,256]{1,0:T(8,128)(2,1)} %bitcast.9, bf16[9,320,320]{2,1,0:T(8,128)(2,1)} %bitcast.5, bf16[9,320,320]{2,1,0:T(8,128)(2,1)} %bitcast.6, bf16[9,320,320]{2,1,0:T(8,128)(2,1)} %bitcast.7, bf16[9,320,320]{2,1,0:T(8,128)(2,1)} %bitcast.8), custom_call_target="tpu_custom_call" | custom-call | tf_op jit(solution)/shard_map/whole/pallas_call | solution.py:472
  44.5 5.2 %copy.10 = f32[64,20480]{1,0:T(8,128)} copy(f32[64,20480]{1,0:T(8,128)} %whole.1) | data formatting | bytes 10485760

commit v3 on v2

--- a/solution.py
+++ b/solution.py
@@ -28,6 +28,14 @@
     return x / (1.0 + jnp.exp(-x))
 
 
+def factors(timestep):
+    angle = jnp.full((8, 128), timestep[0].astype(jnp.float32) * (math.pi / STEPS), jnp.float32)
+    mix = (1.0 + jnp.cos(angle)) * 0.5
+    skip = mix * mix * mix
+    gain = (1.0 - skip) * mix
+    return tuple(v[0:1, 0:1] for v in ((1.0 - mix) / mix, skip / gain, 1.0 - skip, gain))
+
+
 def tap_pieces(parity):
     out = []
     for s in (1, 2, 3):
@@ -47,6 +55,7 @@
 def whole_kernel(
     timestep, fine, coarse_row, coarse_first, coarse_second, local_weight, dilated_weight, out,
     raw, shifted, taps_raw, taps, packed, edges, corner_out, corners, row_in, window_row, patch_in, blocks, acc, staged,
+    lifted, grid, cells1, cells2, cells3, keys, turned,
     in_sem, w_sem, out_sem, send_sem, recv_sem, patch_send, patch_recv,
 ):
     f32, bf = jnp.float32, jnp.bfloat16
@@ -108,33 +117,34 @@
     @pl.when(c == 0)
     def _():
         raw[0:2] = side_zero
-        corners[0] = jnp.zeros((16, PAIR), bf)
-        corners[2] = jnp.zeros((16, PAIR), bf)
+        corners[0] = jnp.zeros((8, PAIR), bf)
+        corners[2] = jnp.zeros((8, PAIR), bf)
 
     @pl.when(c == COLS - 1)
     def _():
         raw[34:36] = side_zero
-        corners[1] = jnp.zeros((16, PAIR), bf)
-        corners[3] = jnp.zeros((16, PAIR), bf)
+        corners[1] = jnp.zeros((8, PAIR), bf)
+        corners[3] = jnp.zeros((8, PAIR), bf)
 
     @pl.when(jnp.logical_not(above))
     def _():
         edges[0] = jnp.zeros((8, 16, PAIR), bf)
-        corners[0] = jnp.zeros((16, PAIR), bf)
-        corners[1] = jnp.zeros((16, PAIR), bf)
-        patch_in[0:3] = jnp.zeros((3, 32, 384), bf)
+        corners[0] = jnp.zeros((8, PAIR), bf)
+        corners[1] = jnp.zeros((8, PAIR), bf)
+        patch_in[0:3] = jnp.zeros((3, 3, 8, 384), bf)
 
     @pl.when(jnp.logical_not(below))
     def _():
         edges[1] = jnp.zeros((8, 16, PAIR), bf)
-        corners[2] = jnp.zeros((16, PAIR), bf)
-        corners[3] = jnp.zeros((16, PAIR), bf)
-        patch_in[19:22] = jnp.zeros((3, 32, 384), bf)
+        corners[2] = jnp.zeros((8, PAIR), bf)
+        corners[3] = jnp.zeros((8, PAIR), bf)
+        patch_in[19:22] = jnp.zeros((3, 3, 8, 384), bf)
 
     row_load.wait()
     turned_row = jnp.concatenate([row_in[...].astype(f32), jnp.zeros((64, 256), f32)], axis=0)
-    window_row[...] = jnp.concatenate(
-        [jnp.zeros((4, 384), f32), jnp.transpose(turned_row), jnp.zeros((28, 384), f32)], axis=0).astype(bf)
+    window = jnp.concatenate(
+        [jnp.zeros((4, 384), f32), jnp.transpose(turned_row), jnp.zeros((12, 384), f32)], axis=0)
+    window_row[...] = window.reshape(34, 8, 384).astype(bf)
     for cp in loads:
         cp.wait()
     for slot, base, first in ((0, 0, 0), (1, 48, 12)):
@@ -145,7 +155,7 @@
             packed[slot, q] = jnp.concatenate([tops[8 * g + q] for g in range(4)], axis=0).astype(bf)
         for k, p in ((0, 30), (1, 0)):
             spot = k if slot == 1 else 2 + k
-            corner_out[spot] = jnp.concatenate([tops[p], tops[p + 1], jnp.zeros((8, PAIR), f32)], axis=0).astype(bf)
+            corner_out[spot] = jnp.concatenate([tops[p], tops[p + 1]], axis=0).astype(bf)
     pl.semaphore_wait(barrier, expected)
 
     last = pl.ds(32, 2)
@@ -173,43 +183,14 @@
             side_copy(k).start()
 
     def window(target):
-        return window_row.at[pl.ds(pl.multiple_of(16 * target, 16), 32), :]
+        return window_row.at[pl.ds(2 * target, 3)]
 
     def patch_copy(dev_r, dev_c, k, slot):
         return pltpu.make_async_remote_copy(
             src_ref=window(dev_c), dst_ref=patch_in.at[k], send_sem=patch_send.at[slot, dev_c],
             recv_sem=patch_recv.at[k], device_id=(dev_r, dev_c), device_id_type=MESH)
 
-    own = pltpu.make_async_copy(window(c), patch_in.at[c + 3], patch_recv.at[c + 3])
-    own.start()
-
-    def send_row(step, _):
-        patch_copy(r, lax.rem(c + step, COLS), c + 3, 0).start()
-        return 0
-
-    lax.fori_loop(1, COLS, send_row, 0)
-
-    @pl.when(down)
-    def _():
-        def one(step, _):
-            patch_copy(r + 1, lax.rem(c + step, COLS), c - 13, 1).start()
-            return 0
-        lax.fori_loop(0, COLS, one, 0)
-
-    @pl.when(up)
-    def _():
-        def one(step, _):
-            patch_copy(r - 1, lax.rem(c + step, COLS), c + 19, 1).start()
-            return 0
-        lax.fori_loop(0, COLS, one, 0)
-
-    angle = jnp.full((8, 128), timestep[0].astype(f32) * (math.pi / STEPS), f32)
-    mix_all = (1.0 + jnp.cos(angle)) * 0.5
-    skip_all = mix_all * mix_all * mix_all
-    gain_all = (1.0 - skip_all) * mix_all
-    one_of = lambda v: v[0:1, 0:1]
-    ratio, lift = one_of((1.0 - mix_all) / mix_all), one_of(skip_all / gain_all)
-    keep, gain = one_of(1.0 - skip_all), one_of(gain_all)
+    ratio, lift, keep, gain = factors(timestep)
 
     for cp in w_loads:
         cp.wait()
@@ -278,53 +259,93 @@
         def _():
             side_copy(k).wait_recv()
 
-    def fine_work(lifted):
-        def first_part(p, _):
-            values = silu(raw[p].astype(f32))
-            lifted[p, 8:72, :] = values
-            shifted[2, p] = values.astype(bf)
-            for k in (0, 1, 3, 4):
-                s = SHIFTS[k]
-                shifted[k, p, 16:48, :] = lifted[p, 24 + s : 56 + s, :].astype(bf)
+    def first_part(p, _):
+        values = silu(raw[p].astype(f32))
+        lifted[p, 8:72, :] = values
+        shifted[2, p] = values.astype(bf)
+        for k in (0, 1, 3, 4):
+            s = SHIFTS[k]
+            shifted[k, p, 16:48, :] = lifted[p, 24 + s : 56 + s, :].astype(bf)
+        return 0
+
+    def second_part(p):
+        for k in (0, 1, 3, 4):
+            s = SHIFTS[k]
+            shifted[k, p, 0:16, :] = lifted[p, 8 + s : 24 + s, :].astype(bf)
+            shifted[k, p, 48:64, :] = lifted[p, 56 + s : 72 + s, :].astype(bf)
+
+    def convolve(h, par, rim, lifts=False):
+        pieces = keys_of(h, par, rim)
+        lhs = taps[par]
+        if lifts:
+            pieces = pieces + [shares(h, par, rim)]
+            lhs = jnp.concatenate([lhs, blocks[h]], axis=1)
+        acc[2 * h + rim, C * par : C * par + C, :] = lax.dot_general(
+            lhs, jnp.concatenate(pieces, axis=1), contract, preferred_element_type=f32)
+
+    def raise_by(h, par, rim):
+        acc[2 * h + rim, C * par : C * par + C, :] += lax.dot_general(
+            blocks[h], shares(h, par, rim), contract, preferred_element_type=f32)
+
+    lax.fori_loop(2, 20, first_part, 0)
+
+    own = pltpu.make_async_copy(window(c), patch_in.at[c + 3], patch_recv.at[c + 3])
+    own.start()
+
+    def send_row(step, _):
+        patch_copy(r, lax.rem(c + step, COLS), c + 3, 0).start()
+        return 0
+
+    lax.fori_loop(1, COLS, send_row, 0)
+
+    @pl.when(down)
+    def _():
+        def one(step, _):
+            patch_copy(r + 1, lax.rem(c + step, COLS), c - 13, 1).start()
             return 0
-
-        lax.fori_loop(2, PAIRS + 2, first_part, 0)
-        arrived(0)
-        arrived(1)
-        for p in (0, 1, 34, 35):
-            first_part(p, 0)
-        for h in range(2):
-            for par in range(2):
-                rhs = jnp.concatenate(keys_of(h, par, False), axis=1)
-                acc[h, C * par : C * par + C, :] = lax.dot_general(taps[par], rhs, contract, preferred_element_type=f32)
-        for k in range(2, 8):
-            arrived(k)
-        for slot, base in ((0, 4), (1, 72)):
-            for q in range(8):
-                block = silu(edges[slot, q].astype(f32))
-                for g in range(4):
-                    lifted[2 + 8 * g + q, base : base + 4, :] = block[4 * g : 4 * g + 4]
-            for k, first in ((0, 0), (1, 34)):
-                block = silu(corners[2 * slot + k].astype(f32))
-                for p in range(2):
-                    lifted[first + p, base : base + 4, :] = block[4 * p : 4 * p + 4]
-
-        def second_part(p, _):
-            for k in (0, 1, 3, 4):
-                s = SHIFTS[k]
-                shifted[k, p, 0:16, :] = lifted[p, 8 + s : 24 + s, :].astype(bf)
-                shifted[k, p, 48:64, :] = lifted[p, 56 + s : 72 + s, :].astype(bf)
+        lax.fori_loop(0, COLS, one, 0)
+
+    @pl.when(up)
+    def _():
+        def one(step, _):
+            patch_copy(r - 1, lax.rem(c + step, COLS), c + 19, 1).start()
             return 0
-
-        lax.fori_loop(0, PAIRS + 4, second_part, 0)
-
-    pl.run_scoped(fine_work, pltpu.VMEM((36, 80, 640), f32))
+        lax.fori_loop(0, COLS, one, 0)
+
+    arrived(0)
+    arrived(1)
+    first_part(0, 0)
+    first_part(1, 0)
+    convolve(0, 0, False)
+    for p in range(20, 28):
+        first_part(p, 0)
+    convolve(0, 1, False)
+    for p in range(28, 36):
+        first_part(p, 0)
+    convolve(1, 0, False)
+    convolve(1, 1, False)
+    for k in range(2, 8):
+        arrived(k)
+    for slot, base in ((0, 4), (1, 72)):
+        for q in range(8):
+            block = silu(edges[slot, q].astype(f32))
+            for g in range(4):
+                lifted[2 + 8 * g + q, base : base + 4, :] = block[4 * g : 4 * g + 4]
+        for k, first in ((0, 0), (1, 34)):
+            block = silu(corners[2 * slot + k].astype(f32))
+            for p in range(2):
+                lifted[first + p, base : base + 4, :] = block[4 * p : 4 * p + 4]
+    for p in range(20):
+        second_part(p)
+    convolve(0, 0, True)
+    for p in range(20, 36):
+        second_part(p)
 
     own.wait()
 
     def got_row(step, _):
         k = lax.rem(c + step, COLS) + 3
-        pltpu.make_async_copy(window_row.at[pl.ds(0, 32), :], patch_in.at[k], patch_recv.at[k]).wait()
+        pltpu.make_async_copy(window_row.at[pl.ds(0, 3)], patch_in.at[k], patch_recv.at[k]).wait()
         return 0
 
     lax.fori_loop(1, COLS, got_row, 0)
@@ -332,68 +353,57 @@
         for cond, slot in ((above, k), (below, 19 + k)):
             @pl.when(cond)
             def _(slot=slot):
-                pltpu.make_async_copy(window_row.at[pl.ds(0, 32), :], patch_in.at[slot], patch_recv.at[slot]).wait()
-
-    def coarse_work(grid, cells1, cells2, cells3, keys, turned):
-        values = patch_in[...].astype(f32).reshape(22 * 32, 384)
-        for t in range(3):
-            grid[t] = silu(values[:, 128 * t : 128 * t + 128])
-        cells1[520:568, :] = jnp.zeros((48, 384), f32)
-        cells2[400:432, :] = jnp.zeros((32, 384), f32)
-        cells3[360:384, :] = jnp.zeros((24, 384), f32)
-        for t in range(3):
-            lanes = slice(128 * t, 128 * t + 128)
-            for m in range(22):
-                cells1[24 * m : 24 * m + 24, lanes] = jnp.concatenate(
-                    [grid[t, pl.ds(m + 1, 22, stride=32), :], jnp.zeros((2, 128), f32)], axis=0)
-        for t in range(3):
-            grid[t] = values[:, 128 * t : 128 * t + 128]
-        for t in range(3):
-            lanes = slice(128 * t, 128 * t + 128)
-            for m in range(18):
-                cells3[PITCH * m : PITCH * m + PITCH, lanes] = grid[t, pl.ds(64 + m + 3, PITCH, stride=32), :]
-        for a in range(3):
-            for b in range(3):
-                k = 3 * a + b
-                first = 24 * b + a
-                keys[:, 384 * k : 384 * k + 384] = cells1[first : first + 512, :].astype(bf)
-        widen = lambda w: jnp.concatenate([w, gap], axis=1)
-        first_taps = jnp.concatenate([widen(taps_raw[2, k]) for k in range(9)], axis=1)
-        hidden = lax.dot_general(first_taps, keys[:, 0:3456], contract, preferred_element_type=f32)
-        hidden = jnp.concatenate([silu(hidden), jnp.zeros((64, 512), f32)], axis=0)
-        turned[...] = jnp.transpose(hidden)
-        field_row = lax.broadcasted_iota(jnp.int32, (PITCH, 384), 0) + (16 * r - 2)
-        row_ok = jnp.logical_and(field_row >= 0, field_row < 128)
-        for m in range(20):
-            col = 16 * c - 2 + m
-            ok = jnp.logical_and(row_ok, jnp.logical_and(col >= 0, col < 256))
-            cells2[PITCH * m : PITCH * m + PITCH, :] = jnp.where(ok, turned[24 * m : 24 * m + PITCH, :], 0.0)
-        for a in range(3):
-            for b in range(3):
-                k = 3 * a + b
-                first = PITCH * b + a
-                keys[0:384, 384 * k : 384 * k + 384] = cells2[first : first + 384, :].astype(bf)
-        keys[0:384, 3456:3840] = cells3[...].astype(bf)
-        eye = lax.broadcasted_iota(jnp.int32, (C, 384), 0) == lax.broadcasted_iota(jnp.int32, (C, 384), 1)
-        second_taps = jnp.concatenate([widen(taps_raw[3, k]) for k in range(9)] + [eye.astype(f32).astype(bf)], axis=1)
-        coarse = lift * lax.dot_general(second_taps, keys[0:384, :], contract, preferred_element_type=f32)
-        for h in range(2):
-            part = coarse if h == 0 else pltpu.roll(coarse, 384 - 160, axis=1)
-            part = part[:, 0:256]
-            high = part.astype(bf)
-            blocks[h, :, 0:256] = high
-            blocks[h, :, 256:512] = (part - high.astype(f32)).astype(bf)
-
-    pl.run_scoped(
-        coarse_work,
-        pltpu.VMEM((3, 704, 128), f32),
-        pltpu.VMEM((568, 384), f32),
-        pltpu.VMEM((432, 384), f32),
-        pltpu.VMEM((384, 384), f32),
-        pltpu.VMEM((512, 3840), bf),
-        pltpu.VMEM((512, 384), f32),
-    )
-
+                pltpu.make_async_copy(window_row.at[pl.ds(0, 3)], patch_in.at[slot], patch_recv.at[slot]).wait()
+
+    values = patch_in[...].astype(f32).reshape(22 * 24, 384)
+    for t in range(3):
+        grid[t] = silu(values[:, 128 * t : 128 * t + 128])
+    cells1[520:568, :] = jnp.zeros((48, 384), f32)
+    cells2[400:432, :] = jnp.zeros((32, 384), f32)
+    cells3[360:384, :] = jnp.zeros((24, 384), f32)
+    for t in range(3):
+        lanes = slice(128 * t, 128 * t + 128)
+        for m in range(22):
+            cells1[24 * m : 24 * m + 24, lanes] = jnp.concatenate(
+                [grid[t, pl.ds(m + 1, 22, stride=24), :], jnp.zeros((2, 128), f32)], axis=0)
+    for t in range(3):
+        grid[t] = values[:, 128 * t : 128 * t + 128]
+    for t in range(3):
+        lanes = slice(128 * t, 128 * t + 128)
+        for m in range(18):
+            cells3[PITCH * m : PITCH * m + PITCH, lanes] = grid[t, pl.ds(48 + m + 3, PITCH, stride=24), :]
+    for a in range(3):
+        for b in range(3):
+            k = 3 * a + b
+            first = 24 * b + a
+            keys[:, 384 * k : 384 * k + 384] = cells1[first : first + 512, :].astype(bf)
+    convolve(0, 1, True)
+    widen = lambda w: jnp.concatenate([w, gap], axis=1)
+    first_taps = jnp.concatenate([widen(taps_raw[2, k]) for k in range(9)], axis=1)
+    hidden = lax.dot_general(first_taps, keys[:, 0:3456], contract, preferred_element_type=f32)
+    hidden = jnp.concatenate([silu(hidden), jnp.zeros((64, 512), f32)], axis=0)
+    turned[...] = jnp.transpose(hidden)
+    field_row = lax.broadcasted_iota(jnp.int32, (PITCH, 384), 0) + (16 * r - 2)
+    row_ok = jnp.logical_and(field_row >= 0, field_row < 128)
+    for m in range(20):
+        col = 16 * c - 2 + m
+        ok = jnp.logical_and(row_ok, jnp.logical_and(col >= 0, col < 256))
+        cells2[PITCH * m : PITCH * m + PITCH, :] = jnp.where(ok, turned[24 * m : 24 * m + PITCH, :], 0.0)
+    for a in range(3):
+        for b in range(3):
+            k = 3 * a + b
+            first = PITCH * b + a
+            keys[0:384, 384 * k : 384 * k + 384] = cells2[first : first + 384, :].astype(bf)
+    keys[0:384, 3456:3840] = cells3[...].astype(bf)
+    eye = lax.broadcasted_iota(jnp.int32, (C, 384), 0) == lax.broadcasted_iota(jnp.int32, (C, 384), 1)
+    second_taps = jnp.concatenate([widen(taps_raw[3, k]) for k in range(9)] + [eye.astype(f32).astype(bf)], axis=1)
+    coarse = lift * lax.dot_general(second_taps, keys[0:384, :], contract, preferred_element_type=f32)
+    for h in range(2):
+        part = coarse if h == 0 else pltpu.roll(coarse, 384 - 160, axis=1)
+        part = part[:, 0:256]
+        high = part.astype(bf)
+        blocks[h, :, 0:256] = high
+        blocks[h, :, 256:512] = (part - high.astype(f32)).astype(bf)
     writes = {}
 
     def blend(h, rim, source, slot):
@@ -421,21 +431,19 @@
             cp.start()
             writes[slot].append(cp)
 
-    for h in range(2):
+    def raised(h, rim):
         for par in range(2):
-            acc[h, C * par : C * par + C, :] += lax.dot_general(
-                blocks[h], shares(h, par, False), contract, preferred_element_type=f32)
-        target = 2 if h == 0 else 0
-        for par in range(2):
-            rhs = jnp.concatenate(keys_of(h, par, True) + [shares(h, par, True)], axis=1)
-            lhs = jnp.concatenate([taps[par], blocks[h]], axis=1)
-            acc[target, C * par : C * par + C, :] = lax.dot_general(lhs, rhs, contract, preferred_element_type=f32)
-        if h == 0:
-            blend(0, False, 0, 0)
-        else:
-            blend(1, False, 1, 1)
-            blend(0, True, 2, 0)
-            blend(1, True, 0, 1)
+            raise_by(h, par, rim)
+
+    raised(0, False)
+    raised(0, True)
+    blend(0, False, 0, 0)
+    convolve(1, 0, True, True)
+    blend(0, True, 1, 1)
+    raised(1, False)
+    blend(1, False, 2, 0)
+    convolve(1, 1, True, True)
+    blend(1, True, 3, 1)
     for group_of in writes.values():
         for cp in group_of:
             cp.wait()
@@ -481,14 +489,21 @@
             pltpu.VMEM((2, C, KEYS), bf),
             pltpu.VMEM((2, 8, 16, 640), bf),
             pltpu.VMEM((2, 8, 16, 640), bf),
-            pltpu.VMEM((4, 16, 640), bf),
-            pltpu.VMEM((4, 16, 640), bf),
+            pltpu.VMEM((4, 8, 640), bf),
+            pltpu.VMEM((4, 8, 640), bf),
             pltpu.VMEM((C, 256), bf),
-            pltpu.VMEM((288, 384), bf),
-            pltpu.VMEM((22, 32, 384), bf),
+            pltpu.VMEM((34, 8, 384), bf),
+            pltpu.VMEM((22, 3, 8, 384), bf),
             pltpu.VMEM((2, C, 512), bf),
-            pltpu.VMEM((3, PAIR, CELLS), f32),
+            pltpu.VMEM((4, PAIR, CELLS), f32),
             pltpu.VMEM((2, 32, PAIR * CHUNK), f32),
+            pltpu.VMEM((36, 80, 640), f32),
+            pltpu.VMEM((3, 528, 128), f32),
+            pltpu.VMEM((568, 384), f32),
+            pltpu.VMEM((432, 384), f32),
+            pltpu.VMEM((384, 384), f32),
+            pltpu.VMEM((512, 3840), bf),
+            pltpu.VMEM((512, 384), f32),
             pltpu.SemaphoreType.DMA((PAIRS + 1,)),
             pltpu.SemaphoreType.DMA((4,)),
             pltpu.SemaphoreType.DMA((4,)),

time: 49.9 us -> 46.4 us (0.930)
  Pallas kernels: 43.9 us -> 40.4 us
    pallas_call x1, Pallas kernels: 43.9 us -> 40.4 us  [whole(): pl.pallas_call(whole_kernel, out_shape=jax.ShapeDtypeStruct((64, 20480),...]
where the time goes in v3:
time: 46.4 us; the launch traced here: 46.3 us
  Pallas kernels  40.4 us (87%)
  local copies, waits for them, and re-layouts  5.22 us (11%)
  between operations  0.66 us (1%)
    pallas_call x1, Pallas kernels, whole(): pl.pallas_call(whole_kernel, out_shape=jax.ShapeDtypeStruct((64, 20480),...  40.4 us
    unnamed x1, local copies, waits for them, and re-layouts  5.22 us

profile of v3, /device:TPU:1, one launch (start us, length us, event | category | flops | bytes accessed | tf_op | source)
XLA Modules:
  0.0 46.3 jit_solution(11794326986751053157)
XLA Ops:
  0.7 40.4 %whole.1 = f32[64,20480]{1,0:T(8,128)} custom-call(s32[1]{0:T(128)S(6)} %copy.9.timestep, bf16[64,20480]{1,0:T(8,128)(2,1)} %fine.1, bf16[320,256]{1,0:T(8,128)(2,1)} %bitcast.9, bf16[9,320,320]{2,1,0:T(8,128)(2,1)} %bitcast.5, bf16[9,320,320]{2,1,0:T(8,128)(2,1)} %bitcast.6, bf16[9,320,320]{2,1,0:T(8,128)(2,1)} %bitcast.7, bf16[9,320,320]{2,1,0:T(8,128)(2,1)} %bitcast.8), custom_call_target="tpu_custom_call" | custom-call | tf_op jit(solution)/shard_map/whole/pallas_call | solution.py:480
  41.1 5.2 %copy.10 = f32[64,20480]{1,0:T(8,128)} copy(f32[64,20480]{1,0:T(8,128)} %whole.1) | data formatting | bytes 10485760

commit v4 on v3

--- a/solution.py
+++ b/solution.py
@@ -25,7 +25,8 @@
 
 
 def silu(x):
-    return x / (1.0 + jnp.exp(-x))
+    half = 0.5 * x
+    return half + half * jnp.tanh(half)
 
 
 def factors(timestep):
@@ -56,15 +57,13 @@
     timestep, fine, coarse_row, coarse_first, coarse_second, local_weight, dilated_weight, out,
     raw, shifted, taps_raw, taps, packed, edges, corner_out, corners, row_in, window_row, patch_in, blocks, acc, staged,
     lifted, grid, cells1, cells2, cells3, keys, turned,
-    in_sem, w_sem, out_sem, send_sem, recv_sem, patch_send, patch_recv,
+    in_sem, w_sem, out_sem, send_sem, recv_sem, patch_send, patch_recv, pass_send, pass_recv,
 ):
     f32, bf = jnp.float32, jnp.bfloat16
     r = lax.axis_index("row")
     c = lax.axis_index("col")
     above = r > 0
     below = r < ROWS - 1
-    down = jnp.logical_and(below, c >= 13)
-    up = jnp.logical_and(above, c < 3)
 
     def present(dr, dc):
         ok = None
@@ -72,32 +71,6 @@
             if need:
                 ok = cond if ok is None else jnp.logical_and(ok, cond)
         return ok
-
-    barrier = pltpu.get_barrier_semaphore()
-
-    def greet(dev):
-        pl.semaphore_signal(barrier, inc=1, device_id=dev, device_id_type=MESH)
-
-    def greet_row(step, _):
-        greet((r, lax.rem(c + step, COLS)))
-        return 0
-
-    lax.fori_loop(1, COLS, greet_row, 0)
-    diagonal = ((-1, -1), (-1, 0), (-1, 1), (1, -1), (1, 0), (1, 1))
-    expected = COLS - 1 + jnp.where(down, COLS, 0) + jnp.where(up, COLS, 0)
-    for step in diagonal:
-        @pl.when(present(*step))
-        def _(step=step):
-            greet((r + step[0], c + step[1]))
-        expected = expected + jnp.where(present(*step), 1, 0)
-    for k in range(3):
-        @pl.when(above)
-        def _(k=k):
-            greet((r - 1, 13 + k))
-
-        @pl.when(below)
-        def _(k=k):
-            greet((r + 1, k))
 
     row_load = pltpu.make_async_copy(coarse_row, row_in, in_sem.at[PAIRS])
     row_load.start()
@@ -106,12 +79,24 @@
         cp = pltpu.make_async_copy(fine.at[:, pl.ds(PAIR * p, PAIR)], raw.at[p + 2], in_sem.at[p])
         cp.start()
         loads.append(cp)
-    w_loads = []
-    for k, ref in enumerate((dilated_weight, local_weight, coarse_first, coarse_second)):
-        cp = pltpu.make_async_copy(ref, taps_raw.at[k], w_sem.at[k])
-        cp.start()
-        w_loads.append(cp)
-
+
+    barrier = pltpu.get_barrier_semaphore()
+
+    def greet(dev):
+        pl.semaphore_signal(barrier, inc=1, device_id=dev, device_id_type=MESH)
+
+    def greet_row(step, _):
+        greet((r, lax.rem(c + step, COLS)))
+        return 0
+
+    lax.fori_loop(1, COLS, greet_row, 0)
+    diagonal = ((-1, -1), (-1, 0), (-1, 1), (1, -1), (1, 0), (1, 1))
+    expected = jnp.int32(COLS - 1)
+    for step in diagonal:
+        @pl.when(present(*step))
+        def _(step=step):
+            greet((r + step[0], c + step[1]))
+        expected = expected + jnp.where(present(*step), 1, 0)
     side_zero = jnp.zeros((2, TALL, PAIR), bf)
 
     @pl.when(c == 0)
@@ -140,13 +125,13 @@
         corners[3] = jnp.zeros((8, PAIR), bf)
         patch_in[19:22] = jnp.zeros((3, 3, 8, 384), bf)
 
-    row_load.wait()
-    turned_row = jnp.concatenate([row_in[...].astype(f32), jnp.zeros((64, 256), f32)], axis=0)
-    window = jnp.concatenate(
-        [jnp.zeros((4, 384), f32), jnp.transpose(turned_row), jnp.zeros((12, 384), f32)], axis=0)
-    window_row[...] = window.reshape(34, 8, 384).astype(bf)
     for cp in loads:
         cp.wait()
+    w_loads = []
+    for k, ref in enumerate((dilated_weight, local_weight, coarse_first, coarse_second)):
+        cp = pltpu.make_async_copy(ref, taps_raw.at[k], w_sem.at[k])
+        cp.start()
+        w_loads.append(cp)
     for slot, base, first in ((0, 0, 0), (1, 48, 12)):
         tops = {}
         for p in range(PAIRS):
@@ -185,11 +170,16 @@
     def window(target):
         return window_row.at[pl.ds(2 * target, 3)]
 
-    def patch_copy(dev_r, dev_c, k, slot):
+    def patch_copy(dev_c):
         return pltpu.make_async_remote_copy(
-            src_ref=window(dev_c), dst_ref=patch_in.at[k], send_sem=patch_send.at[slot, dev_c],
-            recv_sem=patch_recv.at[k], device_id=(dev_r, dev_c), device_id_type=MESH)
-
+            src_ref=window(dev_c), dst_ref=patch_in.at[c + 3], send_sem=patch_send.at[dev_c],
+            recv_sem=patch_recv.at[c + 3], device_id=(r, dev_c), device_id_type=MESH)
+
+    row_load.wait()
+    turned_row = jnp.concatenate([row_in[...].astype(f32), jnp.zeros((64, 256), f32)], axis=0)
+    wide_row = jnp.concatenate(
+        [jnp.zeros((4, 384), f32), jnp.transpose(turned_row), jnp.zeros((12, 384), f32)], axis=0)
+    window_row[...] = wide_row.reshape(34, 8, 384).astype(bf)
     ratio, lift, keep, gain = factors(timestep)
 
     for cp in w_loads:
@@ -197,7 +187,7 @@
     gap = jnp.zeros((C, 64), bf)
     dilated = lambda a, b: taps_raw[0, 3 * a + b]
     local = lambda a, b: (ratio * taps_raw[1, 3 * a + b].astype(f32)).astype(bf)
-    for par in range(2):
+    def fill_taps(par):
         at = 0
         for a in range(3):
             row = []
@@ -216,6 +206,9 @@
                 w = dilated(a, b)
                 taps[par, :, at : at + 384] = jnp.concatenate([w, gap] if par == 0 else [gap, w], axis=1)
                 at += 384
+
+    fill_taps(0)
+
     contract = (((1,), (1,)), ((), ()))
 
     lane = lax.broadcasted_iota(jnp.int32, (TALL, 256), 1)
@@ -293,36 +286,46 @@
     own.start()
 
     def send_row(step, _):
-        patch_copy(r, lax.rem(c + step, COLS), c + 3, 0).start()
+        patch_copy(lax.rem(c + step, COLS)).start()
         return 0
 
     lax.fori_loop(1, COLS, send_row, 0)
-
-    @pl.when(down)
-    def _():
-        def one(step, _):
-            patch_copy(r + 1, lax.rem(c + step, COLS), c - 13, 1).start()
-            return 0
-        lax.fori_loop(0, COLS, one, 0)
-
-    @pl.when(up)
-    def _():
-        def one(step, _):
-            patch_copy(r - 1, lax.rem(c + step, COLS), c + 19, 1).start()
-            return 0
-        lax.fori_loop(0, COLS, one, 0)
+    passes = (
+        (below, 1, patch_in.at[pl.ds(16, 3)], patch_in.at[pl.ds(0, 3)]),
+        (above, -1, patch_in.at[pl.ds(3, 3)], patch_in.at[pl.ds(19, 3)]),
+    )
+
+    def pass_copy(k):
+        cond, step, src, dst = passes[k]
+        return pltpu.make_async_remote_copy(
+            src_ref=src, dst_ref=dst, send_sem=pass_send.at[k], recv_sem=pass_recv.at[k],
+            device_id=(r + step, c), device_id_type=MESH)
 
     arrived(0)
     arrived(1)
     first_part(0, 0)
     first_part(1, 0)
     convolve(0, 0, False)
+    fill_taps(1)
     for p in range(20, 28):
         first_part(p, 0)
     convolve(0, 1, False)
     for p in range(28, 36):
         first_part(p, 0)
     convolve(1, 0, False)
+    own.wait()
+
+    def got_row(step, _):
+        k = lax.rem(c + step, COLS) + 3
+        pltpu.make_async_copy(window_row.at[pl.ds(0, 3)], patch_in.at[k], patch_recv.at[k]).wait()
+        return 0
+
+    lax.fori_loop(1, COLS, got_row, 0)
+    for k in range(2):
+        @pl.when(passes[k][0])
+        def _(k=k):
+            pass_copy(k).start()
+
     convolve(1, 1, False)
     for k in range(2, 8):
         arrived(k)
@@ -341,19 +344,10 @@
     for p in range(20, 36):
         second_part(p)
 
-    own.wait()
-
-    def got_row(step, _):
-        k = lax.rem(c + step, COLS) + 3
-        pltpu.make_async_copy(window_row.at[pl.ds(0, 3)], patch_in.at[k], patch_recv.at[k]).wait()
-        return 0
-
-    lax.fori_loop(1, COLS, got_row, 0)
-    for k in range(3):
-        for cond, slot in ((above, k), (below, 19 + k)):
-            @pl.when(cond)
-            def _(slot=slot):
-                pltpu.make_async_copy(window_row.at[pl.ds(0, 3)], patch_in.at[slot], patch_recv.at[slot]).wait()
+    for k, cond in ((0, above), (1, below)):
+        @pl.when(cond)
+        def _(k=k):
+            pass_copy(k).wait_recv()
 
     values = patch_in[...].astype(f32).reshape(22 * 24, 384)
     for t in range(3):
@@ -454,24 +448,14 @@
             side_copy(k).wait_send()
 
     def sent_row(step, _):
-        patch_copy(r, lax.rem(c + step, COLS), c + 3, 0).wait_send()
+        patch_copy(lax.rem(c + step, COLS)).wait_send()
         return 0
 
     lax.fori_loop(1, COLS, sent_row, 0)
-
-    @pl.when(down)
-    def _():
-        def one(step, _):
-            patch_copy(r + 1, lax.rem(c + step, COLS), c - 13, 1).wait_send()
-            return 0
-        lax.fori_loop(0, COLS, one, 0)
-
-    @pl.when(up)
-    def _():
-        def one(step, _):
-            patch_copy(r - 1, lax.rem(c + step, COLS), c + 19, 1).wait_send()
-            return 0
-        lax.fori_loop(0, COLS, one, 0)
+    for k in range(2):
+        @pl.when(passes[k][0])
+        def _(k=k):
+            pass_copy(k).wait_send()
 
 
 def whole(*arrays):
@@ -509,19 +493,52 @@
             pltpu.SemaphoreType.DMA((4,)),
             pltpu.SemaphoreType.DMA((8,)),
             pltpu.SemaphoreType.DMA((8,)),
-            pltpu.SemaphoreType.DMA((2, COLS)),
+            pltpu.SemaphoreType.DMA((COLS,)),
             pltpu.SemaphoreType.DMA((22,)),
+            pltpu.SemaphoreType.DMA((2,)),
+            pltpu.SemaphoreType.DMA((2,)),
         ],
         compiler_params=pltpu.CompilerParams(collective_id=0, has_side_effects=True, vmem_limit_bytes=VMEM_LIMIT),
         name="whole",
     )(*arrays)
 
 
+def store_kernel(held, out, block, in_sem, out_sem):
+    lanes = [pl.ds(1280 * k, 1280) for k in range(16)]
+    reads = [pltpu.make_async_copy(held.at[:, lanes[k]], block.at[k], in_sem.at[k]) for k in range(16)]
+    writes = [pltpu.make_async_copy(block.at[k], out.at[:, lanes[k]], out_sem.at[k]) for k in range(16)]
+    for cp in reads:
+        cp.start()
+    for k in range(16):
+        reads[k].wait()
+        writes[k].start()
+    for cp in writes:
+        cp.wait()
+
+
+def store(held):
+    any_spec = pl.BlockSpec(memory_space=pl.ANY)
+    return pl.pallas_call(
+        store_kernel,
+        out_shape=jax.ShapeDtypeStruct((64, 20480), jnp.float32),
+        in_specs=[any_spec],
+        out_specs=any_spec,
+        scratch_shapes=[
+            pltpu.VMEM((16, 64, 1280), jnp.float32),
+            pltpu.SemaphoreType.DMA((16,)),
+            pltpu.SemaphoreType.DMA((16,)),
+        ],
+        compiler_params=pltpu.CompilerParams(vmem_limit_bytes=VMEM_LIMIT),
+        name="store",
+    )(held)
+
+
 def on_device(coarse_latent, fine_latent, timestep, coarse_first, coarse_second, local_weight, dilated_weight):
     flat = lambda w: w.reshape(9, C, C)
-    return whole(
+    held = whole(
         timestep, fine_latent, coarse_latent.reshape(C, 256),
         flat(coarse_first), flat(coarse_second), flat(local_weight), flat(dilated_weight))
+    return store(held)
 
 
 def solution(mesh):

time: 46.4 us -> 44.6 us (0.961)
  local copies, waits for them, and re-layouts: 5.22 us -> 0 us
  Pallas kernels: 40.4 us -> 43.6 us
    unnamed x1 -> x0, local copies, waits for them, and re-layouts: 5.22 us -> none
    pallas_call x0 -> x1, Pallas kernels: none -> 4.93 us  [store(): pl.pallas_call(store_kernel, out_shape=jax.ShapeDtypeStruct((64, 20480),...]
    pallas_call x1, Pallas kernels: 40.4 us -> 38.7 us  [whole(): pl.pallas_call(whole_kernel, out_shape=jax.ShapeDtypeStruct((64, 20480),...]
where the time goes in v4:
time: 44.6 us; the launch traced here: 44.5 us
  Pallas kernels  43.6 us (98%)
  between operations  0.84 us (2%)
    pallas_call x1, Pallas kernels, whole(): pl.pallas_call(whole_kernel, out_shape=jax.ShapeDtypeStruct((64, 20480),...  38.7 us
    pallas_call x1, Pallas kernels, store(): pl.pallas_call(store_kernel, out_shape=jax.ShapeDtypeStruct((64, 20480),...  4.93 us

profile of v4, /device:TPU:1, one launch (start us, length us, event | category | flops | bytes accessed | tf_op | source)
XLA Modules:
  0.0 44.5 jit_solution(4956523510642046359)
XLA Ops:
  0.7 38.7 %whole.1.held = f32[64,20480]{1,0:T(8,128)} custom-call(s32[1]{0:T(128)S(6)} %copy.8.timestep, bf16[64,20480]{1,0:T(8,128)(2,1)} %fine.1, bf16[320,256]{1,0:T(8,128)(2,1)} %bitcast.9, bf16[9,320,320]{2,1,0:T(8,128)(2,1)} %bitcast.5, bf16[9,320,320]{2,1,0:T(8,128)(2,1)} %bitcast.6, bf16[9,320,320]{2,1,0:T(8,128)(2,1)} %bitcast.7, bf16[9,320,320]{2,1,0:T(8,128)(2,1)} %bitcast.8), custom_call_target="tpu_custom_call" | custom-call | tf_op jit(solution)/shard_map/whole/pallas_call | solution.py:464
  39.4 4.9 %store.1 = f32[64,20480]{1,0:T(8,128)} custom-call(f32[64,20480]{1,0:T(8,128)} %whole.1.held), custom_call_target="tpu_custom_call" | custom-call | tf_op jit(solution)/shard_map/store/pallas_call | solution.py:521

commit v5 on v4

--- a/solution.py
+++ b/solution.py
@@ -180,6 +180,14 @@
     wide_row = jnp.concatenate(
         [jnp.zeros((4, 384), f32), jnp.transpose(turned_row), jnp.zeros((12, 384), f32)], axis=0)
     window_row[...] = wide_row.reshape(34, 8, 384).astype(bf)
+    own = pltpu.make_async_copy(window(c), patch_in.at[c + 3], patch_recv.at[c + 3])
+    own.start()
+
+    def send_row(step, _):
+        patch_copy(lax.rem(c + step, COLS)).start()
+        return 0
+
+    lax.fori_loop(1, COLS, send_row, 0)
     ratio, lift, keep, gain = factors(timestep)
 
     for cp in w_loads:
@@ -282,14 +290,6 @@
 
     lax.fori_loop(2, 20, first_part, 0)
 
-    own = pltpu.make_async_copy(window(c), patch_in.at[c + 3], patch_recv.at[c + 3])
-    own.start()
-
-    def send_row(step, _):
-        patch_copy(lax.rem(c + step, COLS)).start()
-        return 0
-
-    lax.fori_loop(1, COLS, send_row, 0)
     passes = (
         (below, 1, patch_in.at[pl.ds(16, 3)], patch_in.at[pl.ds(0, 3)]),
         (above, -1, patch_in.at[pl.ds(3, 3)], patch_in.at[pl.ds(19, 3)]),
@@ -313,14 +313,11 @@
     for p in range(28, 36):
         first_part(p, 0)
     convolve(1, 0, False)
-    own.wait()
-
-    def got_row(step, _):
-        k = lax.rem(c + step, COLS) + 3
+    def got(k):
         pltpu.make_async_copy(window_row.at[pl.ds(0, 3)], patch_in.at[k], patch_recv.at[k]).wait()
-        return 0
-
-    lax.fori_loop(1, COLS, got_row, 0)
+
+    for k in (3, 4, 5, 16, 17, 18):
+        got(k)
     for k in range(2):
         @pl.when(passes[k][0])
         def _(k=k):
@@ -344,6 +341,8 @@
     for p in range(20, 36):
         second_part(p)
 
+    for k in range(6, 16):
+        got(k)
     for k, cond in ((0, above), (1, below)):
         @pl.when(cond)
         def _(k=k):

time: 44.6 us -> 44.7 us (level)
  no operation moved by 1% of the time
where the time goes in v5:
time: 44.7 us; the launch traced here: 44.4 us
  Pallas kernels  43.6 us (98%)
  between operations  0.82 us (2%)
    pallas_call x1, Pallas kernels, whole(): pl.pallas_call(whole_kernel, out_shape=jax.ShapeDtypeStruct((64, 20480),...  38.7 us
    pallas_call x1, Pallas kernels, store(): pl.pallas_call(store_kernel, out_shape=jax.ShapeDtypeStruct((64, 20480),...  4.93 us

profile of v5, /device:TPU:1, one launch (start us, length us, event | category | flops | bytes accessed | tf_op | source)
XLA Modules:
  0.0 44.4 jit_solution(2196400534042851806)
XLA Ops:
  0.7 38.7 %whole.1.held = f32[64,20480]{1,0:T(8,128)} custom-call(s32[1]{0:T(128)S(6)} %copy.8.timestep, bf16[64,20480]{1,0:T(8,128)(2,1)} %fine.1, bf16[320,256]{1,0:T(8,128)(2,1)} %bitcast.9, bf16[9,320,320]{2,1,0:T(8,128)(2,1)} %bitcast.5, bf16[9,320,320]{2,1,0:T(8,128)(2,1)} %bitcast.6, bf16[9,320,320]{2,1,0:T(8,128)(2,1)} %bitcast.7, bf16[9,320,320]{2,1,0:T(8,128)(2,1)} %bitcast.8), custom_call_target="tpu_custom_call" | custom-call | tf_op jit(solution)/shard_map/whole/pallas_call | solution.py:463
  39.3 4.9 %store.1 = f32[64,20480]{1,0:T(8,128)} custom-call(f32[64,20480]{1,0:T(8,128)} %whole.1.held), custom_call_target="tpu_custom_call" | custom-call | tf_op jit(solution)/shard_map/store/pallas_call | solution.py:520
